TPU v7x, 32 devices: a whole 2x2x4 slice. The times are simulated.
32 devices in a mesh: dom: 2 (over x), dp: 2 (over core), seq: 8 (over z, y).
Axes of the slice: x: 2, y: 2, z: 4, core: 2. Of those that a mesh axis runs over, the one named last changes fastest.
Arguments:
- queries: bfloat16 [4096, 64, 128], P(('dom', 'dp', 'seq')), parts along dimension 0, may hold values from -1024 to 1024
- out_grad: bfloat16 [4096, 64, 128], P(('dom', 'dp', 'seq')), parts along dimension 0, may hold values from -24 to 24
- cache_keys: float32 [4096, 8, 128], P(('dom', 'dp', 'seq')), parts along dimension 0, may hold values from -12 to 12
- cache_values: float32 [4096, 8, 128], P(('dom', 'dp', 'seq')), parts along dimension 0, may hold values from -6 to 6
- exponents: int32 [4096, 2, 8], P(('dom', 'dp', 'seq')), parts along dimension 0, may hold values from 4 to 6
- outliers: int32 [16, 128], P('dom'), parts along dimension 0, may hold values from 0 to 2047, as said below
Outputs:
- query_grad: bfloat16 [4096, 64, 128], P(('dom', 'dp', 'seq')), parts along dimension 0
- key_grad: float32 [4096, 8, 128], P(('dom', 'dp', 'seq')), parts along dimension 0
- value_grad: float32 [4096, 8, 128], P(('dom', 'dp', 'seq')), parts along dimension 0
There are 2 independent parts, one for each index of `dom`. A program takes and returns all parts, laid end to end along the dimension named above; each array names one. Nothing has to cross between parts.
Inputs may be any that keep to these rules, and one draw needn't show every extreme that they name: `outliers`: each row holds 128 different slot numbers.
All inputs are finite; a program needn't handle non-finite values.
Results may differ from a plain program's by a relative error of at most 0.0062.
Values may be sent and summed in bfloat16 or wider, within the bound.
A program may use at most 128 MiB of HBM per device.

v0:
```python
import math

import jax
import jax.numpy as jnp
from jax import lax
from jax.sharding import PartitionSpec as P


def step_tables(exponent):
    inverse = jnp.zeros(exponent.shape, jnp.float32)
    stepping = jnp.zeros(exponent.shape, jnp.float32)
    for power in range(16):
        hit = exponent == power
        inverse = jnp.where(hit, jnp.float32(2.0**power), inverse)
        stepping = jnp.where(hit, jnp.float32(2.0 ** (-power)), stepping)
    return (inverse, stepping)


def fake_quant(cache_part, exponent, marked):
    inverse, stepping = step_tables(exponent)
    levels = jnp.floor(cache_part * inverse[:, :, None] + 0.5)
    kept = jnp.clip(levels, -128.0, 127.0) * stepping[:, :, None]
    used = jnp.where(marked[:, :, None], cache_part, kept).astype(jnp.bfloat16)
    inside = (levels >= -128.0) & (levels <= 127.0)
    passed = jnp.where(marked[:, :, None] | inside, 1.0, 0.0).astype(jnp.float32)
    return (used, passed)


def outlier_mask(outliers, first_slot, count):
    slot_ids = first_slot + jnp.arange(count, dtype=jnp.int32)
    hits = outliers.T[None, :, :] == slot_ids[:, None, None]
    return jnp.any(hits, axis=1)


def attend(query_rows, grad_rows, keys_used, values_used):
    total_rows, width = query_rows.shape
    row_block = math.gcd(total_rows, 512)
    inv_root = 1.0 / math.sqrt(width)
    query_blocks = query_rows.reshape(total_rows // row_block, row_block, width)
    grad_blocks = grad_rows.reshape(total_rows // row_block, row_block, width)
    zero_acc = jnp.zeros(keys_used.shape, jnp.float32)

    def one_block(carry, pieces):
        key_acc, value_acc = carry
        query_piece, grad_piece = pieces
        scores = (
            lax.dot_general(
                query_piece, keys_used, (((1,), (1,)), ((), ())), preferred_element_type=jnp.float32
            )
            * inv_root
        )
        peaks = jnp.max(scores, axis=1, keepdims=True)
        weights_raw = jnp.exp(scores - peaks)
        probs = weights_raw / jnp.sum(weights_raw, axis=1, keepdims=True)
        probs_low = probs.astype(jnp.bfloat16)
        value_acc = value_acc + lax.dot_general(
            probs_low, grad_piece, (((0,), (0,)), ((), ())), preferred_element_type=jnp.float32
        )
        prob_grad = lax.dot_general(
            grad_piece, values_used, (((1,), (1,)), ((), ())), preferred_element_type=jnp.float32
        )
        row_delta = jnp.sum(probs * prob_grad, axis=1, keepdims=True)
        score_grad = (probs * (prob_grad - row_delta) * inv_root).astype(jnp.bfloat16)
        piece_grad = jnp.dot(score_grad, keys_used, preferred_element_type=jnp.float32).astype(
            jnp.bfloat16
        )
        key_acc = key_acc + lax.dot_general(
            score_grad, query_piece, (((0,), (0,)), ((), ())), preferred_element_type=jnp.float32
        )
        return ((key_acc, value_acc), piece_grad)

    (key_acc, value_acc), query_grads = lax.scan(
        one_block, (zero_acc, zero_acc), (query_blocks, grad_blocks)
    )
    return (query_grads.reshape(total_rows, width), key_acc, value_acc)


def local(queries, out_grad, cache_keys, cache_values, exponents, outliers):
    local_slots = cache_keys.shape[0]
    kv_heads = cache_keys.shape[1]
    tok_local, heads, width = queries.shape
    first_slot = lax.axis_index(("dp", "seq")) * local_slots
    marked = outlier_mask(outliers, first_slot, local_slots)
    key_used, key_pass = fake_quant(cache_keys, exponents[:, 0, :], marked)
    value_used, value_pass = fake_quant(cache_values, exponents[:, 1, :], marked)
    key_all, value_all = (
        lax.all_gather(key_used, ("dp", "seq"), axis=0, tiled=True),
        lax.all_gather(value_used, ("dp", "seq"), axis=0, tiled=True),
    )
    group = heads // kv_heads
    query_by_kv = (
        queries.reshape(tok_local, kv_heads, group, width)
        .transpose(1, 0, 2, 3)
        .reshape(kv_heads, tok_local * group, width)
    )
    grad_by_kv = (
        out_grad.reshape(tok_local, kv_heads, group, width)
        .transpose(1, 0, 2, 3)
        .reshape(kv_heads, tok_local * group, width)
    )

    def one_head(carry, pieces):
        query_part, grad_part, key_part, value_part = pieces
        return (carry, attend(query_part, grad_part, key_part, value_part))

    unused, results = lax.scan(
        one_head,
        jnp.int32(0),
        (query_by_kv, grad_by_kv, key_all.transpose(1, 0, 2), value_all.transpose(1, 0, 2)),
    )
    query_grad_kv, key_terms, value_terms = results
    key_share, value_share = (
        lax.psum_scatter(key_terms, ("dp", "seq"), scatter_dimension=1, tiled=True),
        lax.psum_scatter(value_terms, ("dp", "seq"), scatter_dimension=1, tiled=True),
    )
    key_grad_used = key_share.transpose(1, 0, 2)
    value_grad_used = value_share.transpose(1, 0, 2)
    query_grad = (
        query_grad_kv.reshape(kv_heads, tok_local, group, width)
        .transpose(1, 0, 2, 3)
        .reshape(tok_local, heads, width)
    )
    key_grad = key_grad_used * key_pass
    value_grad = value_grad_used * value_pass
    return (query_grad, key_grad, value_grad)


def solution(mesh):
    return jax.shard_map(
        local,
        mesh=mesh,
        in_specs=(
            P(("dom", "dp", "seq"), None, None),
            P(("dom", "dp", "seq"), None, None),
            P(("dom", "dp", "seq"), None, None),
            P(("dom", "dp", "seq"), None, None),
            P(("dom", "dp", "seq"), None, None),
            P("dom", None),
        ),
        out_specs=(
            P(("dom", "dp", "seq"), None, None),
            P(("dom", "dp", "seq"), None, None),
            P(("dom", "dp", "seq"), None, None),
        ),
        check_vma=False,
    )
```

profile of v0, /device:TPU:0, one launch (start us, length us, event | category | flops | bytes accessed | tf_op | source)
XLA Modules:
  0.0 999.4 jit_solution(3556747470785895294)
XLA Ops:
  8.6 3.1 compare_reduce_fusion
  11.7 2.6 select_convert_fusion
  15.3 4.7 copy_bitcast_fusion.1
  20.0 47.7 %all-gather.5.cloned.1.call-done = bf16[2048,8,128]{2,1,0:T(8,128)(2,1)} async-done(((bf16[128,8,128]{2,1,0:T(8,128)(2,1)}), bf16[2048,8,128]{2,1,0:T(8,128)(2,1)}) %all-gather.5.cloned.1.call-update) | async-done | bytes 4194320 | tf_op jit(solution)/shard_map/all_gather | solution.py:88
  67.7 4.7 copy.40
  72.4 47.2 %all-gather.3.cloned.1.call-done = bf16[2048,8,128]{2,1,0:T(8,128)(2,1)} async-done(((bf16[128,8,128]{2,1,0:T(8,128)(2,1)}), bf16[2048,8,128]{2,1,0:T(8,128)(2,1)}) %all-gather.3.cloned.1.call-update) | async-done | bytes 4194320 | tf_op jit(solution)/shard_map/all_gather | solution.py:87
  119.6 4.7 copy.39
  124.3 654.4 %while.30 = (s32[]{:T(128)}, bf16[8,1024,128]{2,1,0:T(8,128)(2,1)}, f32[8,2048,128]{2,0,1:T(8,128)}, f32[8,2048,128]{2,0,1:T(8,128)}, bf16[8,1024,128]{2,1,0:T(8...) while((s32[]{:T(128)}, bf16[8,1024,128]{2,1,0:T(8,128)(2,1)}, ...), condition=%wide.region_7.8_spmd, body=%wide.region_1.7_spmd.sunk | while | flops 1365309952 | bytes 65690164 | solution.py:106
  124.3 1.8 constant_dynamic-slice_fusion.3
  126.1 2.2 dynamic-slice_bitcast_fusion.3
  128.3 19.4 %while.31 = (s32[]{:T(128)}, f32[2048,128]{1,0:T(8,128)S(1)}, f32[2048,128]{1,0:T(8,128)}, bf16[2,512,128]{2,1,0:T(8,128)(2,1)}, bf16[2,512,128]{2,1,0:T(8,128)(...) while((s32[]{:T(128)}, f32[2048,128]{1,0:T(8,128)S(1)}, ...), condition=%wide.region_6.6_spmd.clone, body=%wide.region_2.5_spmd.clone.sunk | while | flops 1365309952 | bytes 57825612 | solution.py:72
  128.3 1.9 multiply_reduce_fusion.4
  138.0 1.9 multiply_reduce_fusion.4
  149.3 28.4 %dynamic_update_slice.23 = f32[8,2048,128]{2,0,1:T(8,128)} dynamic-update-slice(f32[8,2048,128]{2,0,1:T(8,128)} %get-tuple-element.423, f32[1,2048,128]{2,0,1:T(1,128)S(1)} %bitcast.120, s32[]{:T(128)S(6)} %copy.71, s32[]{:T(128)} %constant.14.clone.1..sunk, s32[]{:T(128)} %constant.14.clone.1..sunk) | dynamic-update-slice | bytes 2097156 | tf_op jit(solution)/shard_map/while/body/jit(dynamic_update_index_in_dim)/dynamic_update_slice | solution.py:106
  177.7 28.4 %dynamic_update_slice.24 = f32[8,2048,128]{2,0,1:T(8,128)} dynamic-update-slice(f32[8,2048,128]{2,0,1:T(8,128)} %get-tuple-element.424, f32[1,2048,128]{2,0,1:T(1,128)} %bitcast.122, s32[]{:T(128)S(6)} %copy.71, s32[]{:T(128)} %constant.14.clone.1..sunk, s32[]{:T(128)} %constant.14.clone.1..sunk) | dynamic-update-slice | bytes 2097156 | tf_op jit(solution)/shard_map/while/body/jit(dynamic_update_index_in_dim)/dynamic_update_slice | solution.py:106
  206.1 1.8 constant_dynamic-slice_fusion.3
  207.9 2.2 dynamic-slice_bitcast_fusion.3
  210.1 19.4 %while.31 = (s32[]{:T(128)}, f32[2048,128]{1,0:T(8,128)S(1)}, f32[2048,128]{1,0:T(8,128)}, bf16[2,512,128]{2,1,0:T(8,128)(2,1)}, bf16[2,512,128]{2,1,0:T(8,128)(...) while((s32[]{:T(128)}, f32[2048,128]{1,0:T(8,128)S(1)}, ...), condition=%wide.region_6.6_spmd.clone, body=%wide.region_2.5_spmd.clone.sunk | while | flops 1365309952 | bytes 57825612 | solution.py:72
  210.1 1.9 multiply_reduce_fusion.4
  219.8 1.9 multiply_reduce_fusion.4
  231.1 28.4 %dynamic_update_slice.23 = f32[8,2048,128]{2,0,1:T(8,128)} dynamic-update-slice(f32[8,2048,128]{2,0,1:T(8,128)} %get-tuple-element.423, f32[1,2048,128]{2,0,1:T(1,128)S(1)} %bitcast.120, s32[]{:T(128)S(6)} %copy.71, s32[]{:T(128)} %constant.14.clone.1..sunk, s32[]{:T(128)} %constant.14.clone.1..sunk) | dynamic-update-slice | bytes 2097156 | tf_op jit(solution)/shard_map/while/body/jit(dynamic_update_index_in_dim)/dynamic_update_slice | solution.py:106
  259.5 28.4 %dynamic_update_slice.24 = f32[8,2048,128]{2,0,1:T(8,128)} dynamic-update-slice(f32[8,2048,128]{2,0,1:T(8,128)} %get-tuple-element.424, f32[1,2048,128]{2,0,1:T(1,128)} %bitcast.122, s32[]{:T(128)S(6)} %copy.71, s32[]{:T(128)} %constant.14.clone.1..sunk, s32[]{:T(128)} %constant.14.clone.1..sunk) | dynamic-update-slice | bytes 2097156 | tf_op jit(solution)/shard_map/while/body/jit(dynamic_update_index_in_dim)/dynamic_update_slice | solution.py:106
  287.9 1.8 constant_dynamic-slice_fusion.3
  289.7 2.2 dynamic-slice_bitcast_fusion.3
  291.9 19.3 %while.31 = (s32[]{:T(128)}, f32[2048,128]{1,0:T(8,128)S(1)}, f32[2048,128]{1,0:T(8,128)}, bf16[2,512,128]{2,1,0:T(8,128)(2,1)}, bf16[2,512,128]{2,1,0:T(8,128)(...) while((s32[]{:T(128)}, f32[2048,128]{1,0:T(8,128)S(1)}, ...), condition=%wide.region_6.6_spmd.clone, body=%wide.region_2.5_spmd.clone.sunk | while | flops 1365309952 | bytes 57825612 | solution.py:72
  291.9 1.9 multiply_reduce_fusion.4
  301.6 1.9 multiply_reduce_fusion.4
  312.9 28.4 %dynamic_update_slice.23 = f32[8,2048,128]{2,0,1:T(8,128)} dynamic-update-slice(f32[8,2048,128]{2,0,1:T(8,128)} %get-tuple-element.423, f32[1,2048,128]{2,0,1:T(1,128)S(1)} %bitcast.120, s32[]{:T(128)S(6)} %copy.71, s32[]{:T(128)} %constant.14.clone.1..sunk, s32[]{:T(128)} %constant.14.clone.1..sunk) | dynamic-update-slice | bytes 2097156 | tf_op jit(solution)/shard_map/while/body/jit(dynamic_update_index_in_dim)/dynamic_update_slice | solution.py:106
  341.3 28.4 %dynamic_update_slice.24 = f32[8,2048,128]{2,0,1:T(8,128)} dynamic-update-slice(f32[8,2048,128]{2,0,1:T(8,128)} %get-tuple-element.424, f32[1,2048,128]{2,0,1:T(1,128)} %bitcast.122, s32[]{:T(128)S(6)} %copy.71, s32[]{:T(128)} %constant.14.clone.1..sunk, s32[]{:T(128)} %constant.14.clone.1..sunk) | dynamic-update-slice | bytes 2097156 | tf_op jit(solution)/shard_map/while/body/jit(dynamic_update_index_in_dim)/dynamic_update_slice | solution.py:106
  371.5 2.2 dynamic-slice_bitcast_fusion.3
  373.7 19.4 %while.31 = (s32[]{:T(128)}, f32[2048,128]{1,0:T(8,128)S(1)}, f32[2048,128]{1,0:T(8,128)}, bf16[2,512,128]{2,1,0:T(8,128)(2,1)}, bf16[2,512,128]{2,1,0:T(8,128)(...) while((s32[]{:T(128)}, f32[2048,128]{1,0:T(8,128)S(1)}, ...), condition=%wide.region_6.6_spmd.clone, body=%wide.region_2.5_spmd.clone.sunk | while | flops 1365309952 | bytes 57825612 | solution.py:72
  373.7 1.9 multiply_reduce_fusion.4
  383.4 1.9 multiply_reduce_fusion.4
  394.7 28.4 %dynamic_update_slice.23 = f32[8,2048,128]{2,0,1:T(8,128)} dynamic-update-slice(f32[8,2048,128]{2,0,1:T(8,128)} %get-tuple-element.423, f32[1,2048,128]{2,0,1:T(1,128)S(1)} %bitcast.120, s32[]{:T(128)S(6)} %copy.71, s32[]{:T(128)} %constant.14.clone.1..sunk, s32[]{:T(128)} %constant.14.clone.1..sunk) | dynamic-update-slice | bytes 2097156 | tf_op jit(solution)/shard_map/while/body/jit(dynamic_update_index_in_dim)/dynamic_update_slice | solution.py:106
  423.1 28.4 %dynamic_update_slice.24 = f32[8,2048,128]{2,0,1:T(8,128)} dynamic-update-slice(f32[8,2048,128]{2,0,1:T(8,128)} %get-tuple-element.424, f32[1,2048,128]{2,0,1:T(1,128)} %bitcast.122, s32[]{:T(128)S(6)} %copy.71, s32[]{:T(128)} %constant.14.clone.1..sunk, s32[]{:T(128)} %constant.14.clone.1..sunk) | dynamic-update-slice | bytes 2097156 | tf_op jit(solution)/shard_map/while/body/jit(dynamic_update_index_in_dim)/dynamic_update_slice | solution.py:106
  451.5 1.8 constant_dynamic-slice_fusion.3
  453.3 2.2 dynamic-slice_bitcast_fusion.3
  455.5 19.4 %while.31 = (s32[]{:T(128)}, f32[2048,128]{1,0:T(8,128)S(1)}, f32[2048,128]{1,0:T(8,128)}, bf16[2,512,128]{2,1,0:T(8,128)(2,1)}, bf16[2,512,128]{2,1,0:T(8,128)(...) while((s32[]{:T(128)}, f32[2048,128]{1,0:T(8,128)S(1)}, ...), condition=%wide.region_6.6_spmd.clone, body=%wide.region_2.5_spmd.clone.sunk | while | flops 1365309952 | bytes 57825612 | solution.py:72
  455.5 1.9 multiply_reduce_fusion.4
  465.2 1.9 multiply_reduce_fusion.4
  476.5 28.4 %dynamic_update_slice.23 = f32[8,2048,128]{2,0,1:T(8,128)} dynamic-update-slice(f32[8,2048,128]{2,0,1:T(8,128)} %get-tuple-element.423, f32[1,2048,128]{2,0,1:T(1,128)S(1)} %bitcast.120, s32[]{:T(128)S(6)} %copy.71, s32[]{:T(128)} %constant.14.clone.1..sunk, s32[]{:T(128)} %constant.14.clone.1..sunk) | dynamic-update-slice | bytes 2097156 | tf_op jit(solution)/shard_map/while/body/jit(dynamic_update_index_in_dim)/dynamic_update_slice | solution.py:106
  504.9 28.4 %dynamic_update_slice.24 = f32[8,2048,128]{2,0,1:T(8,128)} dynamic-update-slice(f32[8,2048,128]{2,0,1:T(8,128)} %get-tuple-element.424, f32[1,2048,128]{2,0,1:T(1,128)} %bitcast.122, s32[]{:T(128)S(6)} %copy.71, s32[]{:T(128)} %constant.14.clone.1..sunk, s32[]{:T(128)} %constant.14.clone.1..sunk) | dynamic-update-slice | bytes 2097156 | tf_op jit(solution)/shard_map/while/body/jit(dynamic_update_index_in_dim)/dynamic_update_slice | solution.py:106
  535.1 2.2 dynamic-slice_bitcast_fusion.3
  537.3 19.4 %while.31 = (s32[]{:T(128)}, f32[2048,128]{1,0:T(8,128)S(1)}, f32[2048,128]{1,0:T(8,128)}, bf16[2,512,128]{2,1,0:T(8,128)(2,1)}, bf16[2,512,128]{2,1,0:T(8,128)(...) while((s32[]{:T(128)}, f32[2048,128]{1,0:T(8,128)S(1)}, ...), condition=%wide.region_6.6_spmd.clone, body=%wide.region_2.5_spmd.clone.sunk | while | flops 1365309952 | bytes 57825612 | solution.py:72
  537.3 1.9 multiply_reduce_fusion.4
  547.0 1.9 multiply_reduce_fusion.4
  558.3 28.4 %dynamic_update_slice.23 = f32[8,2048,128]{2,0,1:T(8,128)} dynamic-update-slice(f32[8,2048,128]{2,0,1:T(8,128)} %get-tuple-element.423, f32[1,2048,128]{2,0,1:T(1,128)S(1)} %bitcast.120, s32[]{:T(128)S(6)} %copy.71, s32[]{:T(128)} %constant.14.clone.1..sunk, s32[]{:T(128)} %constant.14.clone.1..sunk) | dynamic-update-slice | bytes 2097156 | tf_op jit(solution)/shard_map/while/body/jit(dynamic_update_index_in_dim)/dynamic_update_slice | solution.py:106
  586.7 28.4 %dynamic_update_slice.24 = f32[8,2048,128]{2,0,1:T(8,128)} dynamic-update-slice(f32[8,2048,128]{2,0,1:T(8,128)} %get-tuple-element.424, f32[1,2048,128]{2,0,1:T(1,128)} %bitcast.122, s32[]{:T(128)S(6)} %copy.71, s32[]{:T(128)} %constant.14.clone.1..sunk, s32[]{:T(128)} %constant.14.clone.1..sunk) | dynamic-update-slice | bytes 2097156 | tf_op jit(solution)/shard_map/while/body/jit(dynamic_update_index_in_dim)/dynamic_update_slice | solution.py:106
  616.9 2.2 dynamic-slice_bitcast_fusion.3
  619.1 19.4 %while.31 = (s32[]{:T(128)}, f32[2048,128]{1,0:T(8,128)S(1)}, f32[2048,128]{1,0:T(8,128)}, bf16[2,512,128]{2,1,0:T(8,128)(2,1)}, bf16[2,512,128]{2,1,0:T(8,128)(...) while((s32[]{:T(128)}, f32[2048,128]{1,0:T(8,128)S(1)}, ...), condition=%wide.region_6.6_spmd.clone, body=%wide.region_2.5_spmd.clone.sunk | while | flops 1365309952 | bytes 57825612 | solution.py:72
  619.1 1.9 multiply_reduce_fusion.4
  628.8 1.9 multiply_reduce_fusion.4
  640.1 28.4 %dynamic_update_slice.23 = f32[8,2048,128]{2,0,1:T(8,128)} dynamic-update-slice(f32[8,2048,128]{2,0,1:T(8,128)} %get-tuple-element.423, f32[1,2048,128]{2,0,1:T(1,128)S(1)} %bitcast.120, s32[]{:T(128)S(6)} %copy.71, s32[]{:T(128)} %constant.14.clone.1..sunk, s32[]{:T(128)} %constant.14.clone.1..sunk) | dynamic-update-slice | bytes 2097156 | tf_op jit(solution)/shard_map/while/body/jit(dynamic_update_index_in_dim)/dynamic_update_slice | solution.py:106
  668.5 28.4 %dynamic_update_slice.24 = f32[8,2048,128]{2,0,1:T(8,128)} dynamic-update-slice(f32[8,2048,128]{2,0,1:T(8,128)} %get-tuple-element.424, f32[1,2048,128]{2,0,1:T(1,128)} %bitcast.122, s32[]{:T(128)S(6)} %copy.71, s32[]{:T(128)} %constant.14.clone.1..sunk, s32[]{:T(128)} %constant.14.clone.1..sunk) | dynamic-update-slice | bytes 2097156 | tf_op jit(solution)/shard_map/while/body/jit(dynamic_update_index_in_dim)/dynamic_update_slice | solution.py:106
  698.7 2.2 dynamic-slice_bitcast_fusion.3
  700.9 19.4 %while.31 = (s32[]{:T(128)}, f32[2048,128]{1,0:T(8,128)S(1)}, f32[2048,128]{1,0:T(8,128)}, bf16[2,512,128]{2,1,0:T(8,128)(2,1)}, bf16[2,512,128]{2,1,0:T(8,128)(...) while((s32[]{:T(128)}, f32[2048,128]{1,0:T(8,128)S(1)}, ...), condition=%wide.region_6.6_spmd.clone, body=%wide.region_2.5_spmd.clone.sunk | while | flops 1365309952 | bytes 57825612 | solution.py:72
  700.9 1.9 multiply_reduce_fusion.4
  710.6 1.9 multiply_reduce_fusion.4
  721.9 28.4 %dynamic_update_slice.23 = f32[8,2048,128]{2,0,1:T(8,128)} dynamic-update-slice(f32[8,2048,128]{2,0,1:T(8,128)} %get-tuple-element.423, f32[1,2048,128]{2,0,1:T(1,128)S(1)} %bitcast.120, s32[]{:T(128)S(6)} %copy.71, s32[]{:T(128)} %constant.14.clone.1..sunk, s32[]{:T(128)} %constant.14.clone.1..sunk) | dynamic-update-slice | bytes 2097156 | tf_op jit(solution)/shard_map/while/body/jit(dynamic_update_index_in_dim)/dynamic_update_slice | solution.py:106
  750.3 28.4 %dynamic_update_slice.24 = f32[8,2048,128]{2,0,1:T(8,128)} dynamic-update-slice(f32[8,2048,128]{2,0,1:T(8,128)} %get-tuple-element.424, f32[1,2048,128]{2,0,1:T(1,128)} %bitcast.122, s32[]{:T(128)S(6)} %copy.71, s32[]{:T(128)} %constant.14.clone.1..sunk, s32[]{:T(128)} %constant.14.clone.1..sunk) | dynamic-update-slice | bytes 2097156 | tf_op jit(solution)/shard_map/while/body/jit(dynamic_update_index_in_dim)/dynamic_update_slice | solution.py:106
  779.4 3.6 copy_bitcast_fusion
  783.0 99.1 %reduce-scatter.5.cloned.1.call-done = f32[8,128,128]{2,0,1:T(8,128)} async-done(((f32[8,2048,128]{2,0,1:T(8,128)}), f32[8,128,128]{2,0,1:T(8,128)}) %reduce-scatter.5.cloned.1.call-update) | async-done | bytes 524304 | tf_op jit(solution)/shard_map/reduce_scatter | solution.py:114
  882.1 108.4 %reduce-scatter.3.cloned.1.call-done = f32[8,128,128]{2,0,1:T(8,128)} async-done(((f32[8,2048,128]{2,0,1:T(8,128)}), f32[8,128,128]{2,0,1:T(8,128)}) %reduce-scatter.3.cloned.1.call-update) | async-done | bytes 524304 | tf_op jit(solution)/shard_map/reduce_scatter | solution.py:113
  990.5 2.4 bitcast_multiply_fusion
  (393 shorter events, 145.1 us)
Async XLA Ops:
  7.2 8.2 copy-start
  7.2 60.6 %all-gather.5.cloned.1.call-start = ((), (), s32[]{:S(2)}) async-start(), calls=%async_computation.3 | async-start | bytes 4456448 | tf_op jit(solution)/shard_map/all_gather | solution.py:88
  8.2 11.8 %copy-start.10 = (f32[128,8]{1,0:T(8,128)}, f32[128,8]{1,0:T(8,128)S(1)}, u32[]{:S(2)}) copy-start(f32[128,8]{1,0:T(8,128)S(1)} %copy.37) | copy-start | bytes 12292
  8.6 11.4 %copy-start.12 = (f32[128,8]{1,0:T(8,128)}, f32[128,8]{1,0:T(8,128)S(1)}, u32[]{:S(2)}) copy-start(f32[128,8]{1,0:T(8,128)S(1)} %copy.35) | copy-start | bytes 12292
  11.7 2.6 copy-start.14
  14.3 105.3 %all-gather.3.cloned.1.call-start = ((), (), s32[]{:S(2)}) async-start(), calls=%async_computation.2 | async-start | bytes 4456448 | tf_op jit(solution)/shard_map/all_gather | solution.py:87
  15.1 867.0 %reduce-scatter.5.cloned.1.call-start = ((), (), s32[]{:S(2)}) async-start(), calls=%async_computation.5 | async-start | bytes 8912896 | tf_op jit(solution)/shard_map/reduce_scatter | solution.py:114
  128.3 2.8 copy-start.2
  128.3 2.8 copy-start.7
  131.1 1.7 copy-start.4
  138.0 2.8 copy-start.2
  138.0 2.8 copy-start.7
  140.8 1.7 copy-start.4
  142.4 1.6 copy-start.3
  210.1 2.8 copy-start.2
  210.1 2.8 copy-start.7
  212.9 1.7 copy-start.4
  219.8 2.8 copy-start.2
  219.8 2.8 copy-start.7
  222.6 1.7 copy-start.4
  291.9 2.8 copy-start.2
  291.9 2.8 copy-start.7
  294.7 1.7 copy-start.4
  301.6 2.8 copy-start.2
  301.6 2.8 copy-start.7
  304.4 1.7 copy-start.4
  373.7 2.8 copy-start.2
  373.7 2.8 copy-start.7
  376.5 1.7 copy-start.4
  383.4 2.8 copy-start.2
  383.4 2.8 copy-start.7
  386.2 1.7 copy-start.4
  455.5 2.8 copy-start.2
  455.5 2.8 copy-start.7
  458.3 1.7 copy-start.4
  459.9 1.6 copy-start.3
  465.2 2.8 copy-start.2
  465.2 2.8 copy-start.7
  468.0 1.7 copy-start.4
  537.3 2.8 copy-start.2
  537.3 2.8 copy-start.7
  540.1 1.7 copy-start.4
  547.0 2.8 copy-start.2
  547.0 2.8 copy-start.7
  549.8 1.7 copy-start.4
  619.1 2.8 copy-start.2
  619.1 2.8 copy-start.7
  621.9 1.7 copy-start.4
  623.5 1.6 copy-start.3
  628.8 2.8 copy-start.2
  628.8 2.8 copy-start.7
  631.6 1.7 copy-start.4
  700.9 2.8 copy-start.2
  700.9 2.8 copy-start.7
  703.7 1.7 copy-start.4
  710.6 2.8 copy-start.2
  710.6 2.8 copy-start.7
  713.4 1.7 copy-start.4
  778.7 211.7 %reduce-scatter.3.cloned.1.call-start = ((), (), s32[]{:S(2)}) async-start(), calls=%async_computation.4 | async-start | bytes 8912896 | tf_op jit(solution)/shard_map/reduce_scatter | solution.py:113
  779.3 211.2 %copy-start.8 = (f32[128,8,128]{2,1,0:T(8,128)S(1)}, f32[128,8,128]{2,1,0:T(8,128)}, u32[]{:S(2)}) copy-start(f32[128,8,128]{2,1,0:T(8,128)} %param.13) | copy-start | bytes 1572868
  779.3 211.1 %copy-start.9 = (f32[128,8,128]{2,1,0:T(8,128)S(1)}, f32[128,8,128]{2,1,0:T(8,128)}, u32[]{:S(2)}) copy-start(f32[128,8,128]{2,1,0:T(8,128)} %param.12) | copy-start | bytes 1572868
  779.3 211.1 %copy-start.11 = (f32[128,8]{1,0:T(8,128)S(1)}, f32[128,8]{1,0:T(8,128)}, u32[]{:S(2)}) copy-start(f32[128,8]{1,0:T(8,128)} %copy-done.10) | copy-start | bytes 12292
  779.3 211.1 %copy-start.13 = (f32[128,8]{1,0:T(8,128)S(1)}, f32[128,8]{1,0:T(8,128)}, u32[]{:S(2)}) copy-start(f32[128,8]{1,0:T(8,128)} %copy-done.12) | copy-start | bytes 12292
  779.4 211.1 %copy-start.15 = (pred[128,8]{1,0:T(8,128)(4,1)S(1)}, pred[128,8]{1,0:T(8,128)(4,1)}, u32[]{:S(2)}) copy-start(pred[128,8]{1,0:T(8,128)(4,1)} %copy-done.14) | copy-start | bytes 3076
  (61 other events, 90.5 us)
Sparse Core Ops, SparseCore 0:
  14.4 53.2 all-gather.4
  70.5 49.0 all-gather.2
  778.9 103.1 reduce-scatter.4
  886.0 104.4 reduce-scatter.2
where the time goes:
time: 1010 us; the launch traced here: 999 us
  local copies, waits for them, and re-layouts  518 us (51%)
  waiting for transfers between devices  304 us (30%)
  matrix products  114 us (11%)
  other arithmetic  46.7 us (5%)
  between operations  13.9 us (1%)
    dynamic_update_slice x24, local copies, waits for them, and re-layouts, local(): lax.scan(one_head, jnp.int32(0), (query_by_kv, grad_by_kv, key_all.transp...  467 us
    reduce_scatter x1, waiting for transfers between devices, local(): lax.psum_scatter(key_terms, ('dp', 'seq'), scatter_dimension=1, tiled=True)  108 us
    reduce_scatter x1, waiting for transfers between devices, local(): lax.psum_scatter(value_terms, ('dp', 'seq'), scatter_dimension=1, tiled=T...  99.1 us
    all_gather x1, waiting for transfers between devices, local(): lax.all_gather(value_used, ('dp', 'seq'), axis=0, tiled=True)  47.7 us
    all_gather x1, waiting for transfers between devices, local(): lax.all_gather(key_used, ('dp', 'seq'), axis=0, tiled=True)  47.2 us
    dot_general x16, matrix products, one_block(): lax.dot_general(query_piece, keys_used, (((1,), (1,)), ((), ())), preferr...  30.9 us
    dot_general x16, matrix products, one_block(): lax.dot_general(probs_low, grad_piece, (((0,), (0,)), ((), ())), preferre...  26.2 us
    dot_general x16, matrix products, one_block(): lax.dot_general(grad_piece, values_used, (((1,), (1,)), ((), ())), prefer...  26 us
  transfers between devices with their start and end apart: 4, of which 4 were waited for; matrix products, arithmetic and copies ran while one was open for 1% of the time, Pallas kernels for 0%

commit v1 on v0

v1 whole, which is shorter than its diff:
```python
import functools
import math

import jax
import jax.numpy as jnp
from jax import lax
from jax.experimental import pallas as pl
from jax.experimental.pallas import tpu as pltpu
from jax.sharding import PartitionSpec as P

TOKEN_BLOCK = 32
HEADS_PER_CALL = 2


def step_tables(exponent):
    inverse = jnp.zeros(exponent.shape, jnp.float32)
    stepping = jnp.zeros(exponent.shape, jnp.float32)
    for power in range(16):
        hit = exponent == power
        inverse = jnp.where(hit, jnp.float32(2.0**power), inverse)
        stepping = jnp.where(hit, jnp.float32(2.0 ** (-power)), stepping)
    return (inverse, stepping)


def fake_quant(cache_part, exponent, marked):
    inverse, stepping = step_tables(exponent)
    levels = jnp.floor(cache_part * inverse[:, :, None] + 0.5)
    kept = jnp.clip(levels, -128.0, 127.0) * stepping[:, :, None]
    used = jnp.where(marked[:, :, None], cache_part, kept).astype(jnp.bfloat16)
    inside = (levels >= -128.0) & (levels <= 127.0)
    passed = jnp.where(marked[:, :, None] | inside, 1.0, 0.0).astype(jnp.float32)
    return (used, passed)


def outlier_mask(outliers, first_slot, count):
    slot_ids = first_slot + jnp.arange(count, dtype=jnp.int32)
    hits = outliers.T[None, :, :] == slot_ids[:, None, None]
    return jnp.any(hits, axis=1)


def dot(a, b, ca, cb):
    return lax.dot_general(a, b, (((ca,), (cb,)), ((), ())), preferred_element_type=jnp.float32)


def attend_kernel(heads, group, q_ref, g_ref, kv_ref, dq_ref, dkv_ref):
    tb, _, width = q_ref.shape
    devices, _, _, part, _ = kv_ref.shape
    slots = devices * part
    rows = tb * group
    inv_root = 1.0 / math.sqrt(width)
    to_exp2 = inv_root * math.log2(math.e)
    q_all = q_ref[...].astype(jnp.float32)
    g_all = g_ref[...].astype(jnp.float32)
    first = pl.program_id(0) == 0
    outs = []
    for h in range(heads):
        q = q_all[:, h * group : (h + 1) * group].reshape(rows, width).astype(jnp.bfloat16)
        g = g_all[:, h * group : (h + 1) * group].reshape(rows, width).astype(jnp.bfloat16)
        k = kv_ref[:, h, 0].reshape(slots, width)
        v = kv_ref[:, h, 1].reshape(slots, width)
        s = dot(k, q, 1, 1)
        peak = jnp.max(s, axis=0, keepdims=True)
        e = jnp.exp2((s - peak) * to_exp2)
        total = jnp.sum(e, axis=0, keepdims=True)
        dp = dot(v, g, 1, 1)
        inv = 1.0 / total
        delta = jnp.sum(e * dp, axis=0, keepdims=True) * inv
        p = e * inv
        dv = dot(p.astype(jnp.bfloat16), g, 1, 0).reshape(devices, part, width)
        ds = (p * (dp - delta)).astype(jnp.bfloat16)
        dk = (dot(ds, q, 1, 0) * inv_root).reshape(devices, part, width)
        dq = dot(k, ds, 0, 0) * inv_root
        outs.append(dq.T.reshape(tb, group, width))

        @pl.when(first)
        def _():
            dkv_ref[:, h, 0] = dk
            dkv_ref[:, h, 1] = dv

        @pl.when(jnp.logical_not(first))
        def _():
            dkv_ref[:, h, 0] += dk
            dkv_ref[:, h, 1] += dv

    dq_ref[...] = jnp.concatenate(outs, axis=1).astype(dq_ref.dtype)


def attend_call(index, heads, group, queries, out_grad, kv_all):
    tokens, _, width = queries.shape
    devices, _, _, part, _ = kv_all.shape
    tb = math.gcd(tokens, TOKEN_BLOCK)
    wide = heads * group
    flops = 10 * tokens * wide * devices * part * width
    return pl.pallas_call(
        functools.partial(attend_kernel, heads, group),
        grid=(tokens // tb,),
        in_specs=[
            pl.BlockSpec((tb, wide, width), lambda i: (i, index, 0)),
            pl.BlockSpec((tb, wide, width), lambda i: (i, index, 0)),
            pl.BlockSpec(kv_all.shape, lambda i: (0, 0, 0, 0, 0)),
        ],
        out_specs=[
            pl.BlockSpec((tb, wide, width), lambda i: (i, 0, 0)),
            pl.BlockSpec(kv_all.shape, lambda i: (0, 0, 0, 0, 0)),
        ],
        out_shape=[
            jax.ShapeDtypeStruct((tokens, wide, width), jnp.bfloat16),
            jax.ShapeDtypeStruct(kv_all.shape, jnp.float32),
        ],
        compiler_params=pltpu.CompilerParams(vmem_limit_bytes=56 << 20),
        cost_estimate=pl.CostEstimate(
            flops=2 * flops, bytes_accessed=12 << 20, transcendentals=tokens * wide * devices * part
        ),
    )(queries, out_grad, kv_all)


def local(queries, out_grad, cache_keys, cache_values, exponents, outliers):
    local_slots, kv_heads, width = cache_keys.shape
    heads = queries.shape[1]
    group = heads // kv_heads
    axes = ("dp", "seq")
    first_slot = lax.axis_index(axes) * local_slots
    marked = outlier_mask(outliers, first_slot, local_slots)
    key_used, key_pass = fake_quant(cache_keys, exponents[:, 0, :], marked)
    value_used, value_pass = fake_quant(cache_values, exponents[:, 1, :], marked)
    kv = jnp.stack([key_used, value_used], axis=0).transpose(2, 0, 1, 3)
    n = HEADS_PER_CALL
    query_grads, shares = [], []
    for c in range(kv_heads // n):
        kv_all = lax.all_gather(kv[c * n : (c + 1) * n], axes, axis=0, tiled=False)
        dq, dkv = attend_call(c, n, group, queries, out_grad, kv_all)
        query_grads.append(dq)
        shares.append(lax.psum_scatter(dkv, axes, scatter_dimension=0, tiled=False))
    query_grad = jnp.concatenate(query_grads, axis=1)
    share = jnp.concatenate(shares, axis=0).transpose(1, 2, 0, 3)
    return (query_grad, share[0] * key_pass, share[1] * value_pass)


def solution(mesh):
    split = P(("dom", "dp", "seq"), None, None)
    return jax.shard_map(
        local,
        mesh=mesh,
        in_specs=(split, split, split, split, split, P("dom", None)),
        out_specs=(split, split, split),
        check_vma=False,
    )
```

time: 1010 us -> 499 us (0.49); the launches traced: 999 us -> 499 us
  local copies, waits for them, and re-layouts: 518 us -> 17.2 us
  matrix products: 114 us -> 0 us
  Pallas kernels: 0 us -> 107 us
  waiting for transfers between devices: 304 us -> 350 us
  other arithmetic: 46.7 us -> 9.43 us
    dynamic_update_slice x24 -> x0, local copies, waits for them, and re-layouts: 467 us -> none  [local(): lax.scan(one_head, jnp.int32(0), (query_by_kv, grad_by_kv, key_all.transp...]
    dot_general x80 -> x0, matrix products: 114 us -> none  [the longest x16 30.9 us: one_block(): lax.dot_general(query_piece, keys_used, (((1,), (1,)), ((), ())), preferr...]
    pallas_call x0 -> x4, Pallas kernels: none -> 107 us  [attend_call(): pl.pallas_call(functools.partial(attend_kernel, heads, group), grid=(toke...]
    reduce_scatter x2 -> x4, waiting for transfers between devices: 207 us -> 268 us  [local(): shares.append(lax.psum_scatter(dkv, axes, scatter_dimension=0, tiled=False))]
    convert_element_type x17 -> x0, other arithmetic: 27 us -> none  [the longest x16 24.5 us: one_block(): (probs * (prob_grad - row_delta) * inv_root).astype(jnp.bfloat16)]
    squeeze x8 -> x0, local copies, waits for them, and re-layouts: 17.9 us -> none  [local(): lax.scan(one_head, jnp.int32(0), (query_by_kv, grad_by_kv, key_all.transp...]
    all_gather x2 -> x4, waiting for transfers between devices: 94.9 us -> 79.6 us  [local(): kv_all = lax.all_gather(kv[c * n:(c + 1) * n], axes, axis=0, tiled=False)]
    dynamic_slice x8 -> x0, local copies, waits for them, and re-layouts: 14.1 us -> none  [local(): lax.scan(one_head, jnp.int32(0), (query_by_kv, grad_by_kv, key_all.transp...]
  transfers between devices with their start and end apart: 4 -> 8, of which waited for: 4 -> 8; matrix products, arithmetic and copies ran while one was open for 1% -> 3% of each run, Pallas kernels for 0% -> 21%
where the time goes in v1:
time: 499 us
  waiting for transfers between devices  350 us (70%)
  Pallas kernels  107 us (21%)
  local copies, waits for them, and re-layouts  17.2 us (3%)
  between operations  14.2 us (3%)
  other arithmetic  9.43 us (2%)
    reduce_scatter x4, waiting for transfers between devices, local(): shares.append(lax.psum_scatter(dkv, axes, scatter_dimension=0, tiled=False))  268 us
    pallas_call x4, Pallas kernels, attend_call(): pl.pallas_call(functools.partial(attend_kernel, heads, group), grid=(toke...  107 us
    all_gather x4, waiting for transfers between devices, local(): kv_all = lax.all_gather(kv[c * n:(c + 1) * n], axes, axis=0, tiled=False)  79.6 us
    all_gather x4, local copies, waits for them, and re-layouts, local(): kv_all = lax.all_gather(kv[c * n:(c + 1) * n], axes, axis=0, tiled=False)  12.6 us
  transfers between devices with their start and end apart: 8, of which 8 were waited for; matrix products, arithmetic and copies ran while one was open for 3% of the time, Pallas kernels for 21%

profile of v1, /device:TPU:0, one launch (start us, length us, event | category | flops | bytes accessed | tf_op | source)
XLA Modules:
  0.0 498.9 jit_solution(8368995006037499957)
XLA Ops:
  7.2 0.0 all-gather.9.cloned.1.call-start
  7.2 0.8 fusion.24
  8.0 3.1 compare_reduce_fusion
  11.1 0.1 copy.21
  11.2 1.9 fusion.8
  13.1 0.1 maximum_bitcast_fusion.1
  13.2 0.8 fusion.70
  14.0 0.0 all-gather.9.cloned.1.call-update
  14.0 0.0 all-gather.11.cloned.1.call-start
  14.1 0.7 all-gather.11.cloned.1.call-update
  14.8 0.0 all-gather.13.cloned.1.call-start
  14.8 0.7 all-gather.13.cloned.1.call-update
  15.5 0.0 all-gather.15.cloned.1.call-start
  15.5 0.5 all-gather.15.cloned.1.call-update
  16.1 0.0 reduce-scatter.5.cloned.1.call-start
  16.1 42.1 %all-gather.9.cloned.1.call-done = bf16[32,2,128,128]{3,2,0,1:T(8,128)(2,1)} async-done(((bf16[2,2,128,128]{3,2,0,1:T(8,128)(2,1)}), bf16[32,2,128,128]{3,2,0,1:T(8,128)(2,1)}) %all-gather.9.cloned.1.call-update) | async-done | bytes 2097168 | tf_op jit(solution)/shard_map/all_gather | solution.py:130
  58.2 3.2 copy.26.kv_ref
  61.4 26.8 %shard_map.85 = (bf16[128,16,128]{2,1,0:T(8,128)(2,1)}, f32[16,2,2,128,128]{4,3,2,1,0:T(8,128)}) custom-call(bf16[128,64,128]{2,1,0:T(8,128)(2,1)} %q_ref.7, bf16[128,64,128]{2,1,0:T(8,128)(2,1)} %g_ref.7, bf16[16,2,2,128,128]{4,3,2,1,0:T(8,128)(2,1)} %copy.26.kv_ref), custom_call_target="tpu_custom_call" | custom-call | flops 10737418240 | bytes 12582912 | tf_op jit(solution)/shard_map/pallas_call | solution.py:94
  88.1 0.0 reduce-scatter.5.cloned.1.call-update
  88.2 0.2 reduce-scatter.7.cloned.1.call-start
  88.4 12.3 %all-gather.11.cloned.1.call-done = bf16[32,2,128,128]{3,2,0,1:T(8,128)(2,1)} async-done(((bf16[2,2,128,128]{3,2,0,1:T(8,128)(2,1)}), bf16[32,2,128,128]{3,2,0,1:T(8,128)(2,1)}) %all-gather.11.cloned.1.call-update) | async-done | bytes 2097168 | tf_op jit(solution)/shard_map/all_gather | solution.py:130
  100.7 3.2 copy.27.kv_ref
  103.9 26.8 %shard_map.86 = (bf16[128,16,128]{2,1,0:T(8,128)(2,1)}, f32[16,2,2,128,128]{4,3,2,1,0:T(8,128)}) custom-call(bf16[128,64,128]{2,1,0:T(8,128)(2,1)} %q_ref.7, bf16[128,64,128]{2,1,0:T(8,128)(2,1)} %g_ref.7, bf16[16,2,2,128,128]{4,3,2,1,0:T(8,128)(2,1)} %copy.27.kv_ref), custom_call_target="tpu_custom_call" | custom-call | flops 10737418240 | bytes 12582912 | tf_op jit(solution)/shard_map/pallas_call | solution.py:94
  130.7 0.0 reduce-scatter.7.cloned.1.call-update
  130.8 0.0 reduce-scatter.9.cloned.1.call-start
  130.8 13.0 %all-gather.13.cloned.1.call-done = bf16[32,2,128,128]{3,2,0,1:T(8,128)(2,1)} async-done(((bf16[2,2,128,128]{3,2,0,1:T(8,128)(2,1)}), bf16[32,2,128,128]{3,2,0,1:T(8,128)(2,1)}) %all-gather.13.cloned.1.call-update) | async-done | bytes 2097168 | tf_op jit(solution)/shard_map/all_gather | solution.py:130
  143.8 3.2 copy.28.kv_ref
  146.9 26.8 %shard_map.87 = (bf16[128,16,128]{2,1,0:T(8,128)(2,1)}, f32[16,2,2,128,128]{4,3,2,1,0:T(8,128)}) custom-call(bf16[128,64,128]{2,1,0:T(8,128)(2,1)} %q_ref.7, bf16[128,64,128]{2,1,0:T(8,128)(2,1)} %g_ref.7, bf16[16,2,2,128,128]{4,3,2,1,0:T(8,128)(2,1)} %copy.28.kv_ref), custom_call_target="tpu_custom_call" | custom-call | flops 10737418240 | bytes 12582912 | tf_op jit(solution)/shard_map/pallas_call | solution.py:94
  173.7 0.0 reduce-scatter.9.cloned.1.call-update
  173.8 0.3 reduce-scatter.11.cloned.1.call-start
  174.0 12.2 %all-gather.15.cloned.1.call-done = bf16[32,2,128,128]{3,2,0,1:T(8,128)(2,1)} async-done(((bf16[2,2,128,128]{3,2,0,1:T(8,128)(2,1)}), bf16[32,2,128,128]{3,2,0,1:T(8,128)(2,1)}) %all-gather.15.cloned.1.call-update) | async-done | bytes 2097168 | tf_op jit(solution)/shard_map/all_gather | solution.py:130
  186.2 3.2 copy.29
  189.4 26.8 %shard_map.88 = (bf16[128,16,128]{2,1,0:T(8,128)(2,1)}, f32[16,2,2,128,128]{4,3,2,1,0:T(8,128)}) custom-call(bf16[128,64,128]{2,1,0:T(8,128)(2,1)} %q_ref.7, bf16[128,64,128]{2,1,0:T(8,128)(2,1)} %g_ref.7, bf16[16,2,2,128,128]{4,3,2,1,0:T(8,128)(2,1)} %bitcast.52), custom_call_target="tpu_custom_call" | custom-call | flops 10737418240 | bytes 12582912 | tf_op jit(solution)/shard_map/pallas_call | solution.py:94
  216.2 0.0 copy-start.2
  216.2 0.0 copy-start.3
  216.2 0.0 copy-start.4
  216.2 0.0 copy-start.5
  216.2 0.0 reduce-scatter.11.cloned.1.call-update
  216.3 1.0 copy-done.2
  217.3 0.2 copy-done.3
  217.4 0.2 copy-done.4
  217.6 0.2 copy-done.5
  217.7 1.6 pad_maximum_fusion
  219.3 0.0 copy-start
  219.3 0.0 copy-start.1
  219.3 41.6 %reduce-scatter.5.cloned.1.call-done = f32[1,2,2,128,128]{4,3,2,1,0:T(8,128)} async-done(((f32[16,2,2,128,128]{4,3,2,1,0:T(8,128)}), f32[1,2,2,128,128]{4,3,2,1,0:T(8,128)}) %reduce-scatter.5.cloned.1.call-update) | async-done | bytes 262160 | tf_op jit(solution)/shard_map/reduce_scatter | solution.py:133
  260.9 75.8 %reduce-scatter.7.cloned.1.call-done = f32[1,2,2,128,128]{4,3,2,1,0:T(8,128)} async-done(((f32[16,2,2,128,128]{4,3,2,1,0:T(8,128)}), f32[1,2,2,128,128]{4,3,2,1,0:T(8,128)}) %reduce-scatter.7.cloned.1.call-update) | async-done | bytes 262160 | tf_op jit(solution)/shard_map/reduce_scatter | solution.py:133
  336.7 75.2 %reduce-scatter.9.cloned.1.call-done = f32[1,2,2,128,128]{4,3,2,1,0:T(8,128)} async-done(((f32[16,2,2,128,128]{4,3,2,1,0:T(8,128)}), f32[1,2,2,128,128]{4,3,2,1,0:T(8,128)}) %reduce-scatter.9.cloned.1.call-update) | async-done | bytes 262160 | tf_op jit(solution)/shard_map/reduce_scatter | solution.py:133
  411.9 76.0 %reduce-scatter.11.cloned.1.call-done = f32[1,2,2,128,128]{4,3,2,1,0:T(8,128)} async-done(((f32[16,2,2,128,128]{4,3,2,1,0:T(8,128)}), f32[1,2,2,128,128]{4,3,2,1,0:T(8,128)}) %reduce-scatter.11.cloned.1.call-update) | async-done | bytes 262160 | tf_op jit(solution)/shard_map/reduce_scatter | solution.py:133
  487.8 1.3 maximum_bitcast_fusion
  489.1 0.0 copy-done
  489.1 0.0 copy-done.1
  489.1 0.7 fusion
  489.9 1.1 copy.31
  491.0 1.1 copy.32
  (3 shorter events, 0.1 us)
Async XLA Ops:
  7.2 51.0 %all-gather.9.cloned.1.call-start = ((), (), s32[]{:S(2)}) async-start(), calls=%async_computation.8 | async-start | bytes 2228224 | tf_op jit(solution)/shard_map/all_gather | solution.py:130
  14.0 86.7 %all-gather.11.cloned.1.call-start = ((), (), s32[]{:S(2)}) async-start(), calls=%async_computation.9 | async-start | bytes 2228224 | tf_op jit(solution)/shard_map/all_gather | solution.py:130
  14.8 129.0 %all-gather.13.cloned.1.call-start = ((), (), s32[]{:S(2)}) async-start(), calls=%async_computation.10 | async-start | bytes 2228224 | tf_op jit(solution)/shard_map/all_gather | solution.py:130
  15.5 170.7 %all-gather.15.cloned.1.call-start = ((), (), s32[]{:S(2)}) async-start(), calls=%async_computation.11 | async-start | bytes 2228224 | tf_op jit(solution)/shard_map/all_gather | solution.py:130
  16.1 244.9 %reduce-scatter.5.cloned.1.call-start = ((), (), s32[]{:S(2)}) async-start(), calls=%async_computation.4 | async-start | bytes 4456448 | tf_op jit(solution)/shard_map/reduce_scatter | solution.py:133
  88.2 248.6 %reduce-scatter.7.cloned.1.call-start = ((), (), s32[]{:S(2)}) async-start(), calls=%async_computation.5 | async-start | bytes 4456448 | tf_op jit(solution)/shard_map/reduce_scatter | solution.py:133
  130.8 281.1 %reduce-scatter.9.cloned.1.call-start = ((), (), s32[]{:S(2)}) async-start(), calls=%async_computation.6 | async-start | bytes 4456448 | tf_op jit(solution)/shard_map/reduce_scatter | solution.py:133
  173.8 314.1 %reduce-scatter.11.cloned.1.call-start = ((), (), s32[]{:S(2)}) async-start(), calls=%async_computation.7 | async-start | bytes 4456448 | tf_op jit(solution)/shard_map/reduce_scatter | solution.py:133
  216.2 1.0 copy-start.2
  216.2 1.2 copy-start.3
  216.2 1.4 copy-start.4
  216.2 1.5 copy-start.5
  219.3 269.8 %copy-start = (f32[128,8,128]{2,1,0:T(8,128)S(1)}, f32[128,8,128]{2,1,0:T(8,128)}, u32[]{:S(2)}) copy-start(f32[128,8,128]{2,1,0:T(8,128)} %param.8) | copy-start | bytes 1572868
  219.3 269.8 %copy-start.1 = (f32[128,8,128]{2,1,0:T(8,128)S(1)}, f32[128,8,128]{2,1,0:T(8,128)}, u32[]{:S(2)}) copy-start(f32[128,8,128]{2,1,0:T(8,128)} %param.9) | copy-start | bytes 1572868
Sparse Core Ops, SparseCore 0:
  14.1 44.0 all-gather.8
  60.4 40.2 all-gather.10
  103.5 40.1 all-gather.12
  145.9 40.3 all-gather.14
  189.9 70.9 reduce-scatter.4
  265.1 71.5 reduce-scatter.6
  340.6 71.2 reduce-scatter.8
  416.2 71.5 reduce-scatter.10

commit v2 on v1

--- a/solution.py
+++ b/solution.py
@@ -42,10 +42,10 @@
     return lax.dot_general(a, b, (((ca,), (cb,)), ((), ())), preferred_element_type=jnp.float32)
 
 
-def attend_kernel(heads, group, q_ref, g_ref, kv_ref, dq_ref, dkv_ref):
+def attend_kernel(heads, group, q_ref, g_ref, own_ref, other_ref, dq_ref, down_ref, dother_ref):
     tb, _, width = q_ref.shape
-    devices, _, _, part, _ = kv_ref.shape
-    slots = devices * part
+    devices, _, _, part, _ = own_ref.shape
+    half = devices * part
     rows = tb * group
     inv_root = 1.0 / math.sqrt(width)
     to_exp2 = inv_root * math.log2(math.e)
@@ -56,8 +56,12 @@
     for h in range(heads):
         q = q_all[:, h * group : (h + 1) * group].reshape(rows, width).astype(jnp.bfloat16)
         g = g_all[:, h * group : (h + 1) * group].reshape(rows, width).astype(jnp.bfloat16)
-        k = kv_ref[:, h, 0].reshape(slots, width)
-        v = kv_ref[:, h, 1].reshape(slots, width)
+        k = jnp.concatenate(
+            [own_ref[:, h, 0].reshape(half, width), other_ref[:, h, 0].reshape(half, width)], axis=0
+        )
+        v = jnp.concatenate(
+            [own_ref[:, h, 1].reshape(half, width), other_ref[:, h, 1].reshape(half, width)], axis=0
+        )
         s = dot(k, q, 1, 1)
         peak = jnp.max(s, axis=0, keepdims=True)
         e = jnp.exp2((s - peak) * to_exp2)
@@ -66,52 +70,57 @@
         inv = 1.0 / total
         delta = jnp.sum(e * dp, axis=0, keepdims=True) * inv
         p = e * inv
-        dv = dot(p.astype(jnp.bfloat16), g, 1, 0).reshape(devices, part, width)
+        dv = dot(p.astype(jnp.bfloat16), g, 1, 0).reshape(2, devices, part, width)
         ds = (p * (dp - delta)).astype(jnp.bfloat16)
-        dk = (dot(ds, q, 1, 0) * inv_root).reshape(devices, part, width)
+        dk = (dot(ds, q, 1, 0) * inv_root).reshape(2, devices, part, width)
         dq = dot(k, ds, 0, 0) * inv_root
         outs.append(dq.T.reshape(tb, group, width))
 
         @pl.when(first)
         def _():
-            dkv_ref[:, h, 0] = dk
-            dkv_ref[:, h, 1] = dv
+            for side, ref in enumerate((down_ref, dother_ref)):
+                ref[:, h, 0] = dk[side]
+                ref[:, h, 1] = dv[side]
 
         @pl.when(jnp.logical_not(first))
         def _():
-            dkv_ref[:, h, 0] += dk
-            dkv_ref[:, h, 1] += dv
+            for side, ref in enumerate((down_ref, dother_ref)):
+                ref[:, h, 0] += dk[side]
+                ref[:, h, 1] += dv[side]
 
     dq_ref[...] = jnp.concatenate(outs, axis=1).astype(dq_ref.dtype)
 
 
-def attend_call(index, heads, group, queries, out_grad, kv_all):
+def attend_call(index, heads, group, queries, out_grad, own, other):
     tokens, _, width = queries.shape
-    devices, _, _, part, _ = kv_all.shape
+    devices, _, _, part, _ = own.shape
     tb = math.gcd(tokens, TOKEN_BLOCK)
     wide = heads * group
-    flops = 10 * tokens * wide * devices * part * width
+    flops = 20 * tokens * wide * devices * part * width
     return pl.pallas_call(
         functools.partial(attend_kernel, heads, group),
         grid=(tokens // tb,),
         in_specs=[
             pl.BlockSpec((tb, wide, width), lambda i: (i, index, 0)),
             pl.BlockSpec((tb, wide, width), lambda i: (i, index, 0)),
-            pl.BlockSpec(kv_all.shape, lambda i: (0, 0, 0, 0, 0)),
+            pl.BlockSpec(own.shape, lambda i: (0, 0, 0, 0, 0)),
+            pl.BlockSpec(own.shape, lambda i: (0, 0, 0, 0, 0)),
         ],
         out_specs=[
             pl.BlockSpec((tb, wide, width), lambda i: (i, 0, 0)),
-            pl.BlockSpec(kv_all.shape, lambda i: (0, 0, 0, 0, 0)),
+            pl.BlockSpec(own.shape, lambda i: (0, 0, 0, 0, 0)),
+            pl.BlockSpec(own.shape, lambda i: (0, 0, 0, 0, 0)),
         ],
         out_shape=[
             jax.ShapeDtypeStruct((tokens, wide, width), jnp.bfloat16),
-            jax.ShapeDtypeStruct(kv_all.shape, jnp.float32),
+            jax.ShapeDtypeStruct(own.shape, jnp.float32),
+            jax.ShapeDtypeStruct(own.shape, jnp.float32),
         ],
         compiler_params=pltpu.CompilerParams(vmem_limit_bytes=56 << 20),
         cost_estimate=pl.CostEstimate(
-            flops=2 * flops, bytes_accessed=12 << 20, transcendentals=tokens * wide * devices * part
+            flops=2 * flops, bytes_accessed=12 << 20, transcendentals=2 * tokens * wide * devices * part
         ),
-    )(queries, out_grad, kv_all)
+    )(queries, out_grad, own, other)
 
 
 def local(queries, out_grad, cache_keys, cache_values, exponents, outliers):
@@ -126,11 +135,22 @@
     kv = jnp.stack([key_used, value_used], axis=0).transpose(2, 0, 1, 3)
     n = HEADS_PER_CALL
     query_grads, shares = [], []
+    swap = [(0, 1), (1, 0)]
+    block = (n, 2, local_slots, width)
     for c in range(kv_heads // n):
-        kv_all = lax.all_gather(kv[c * n : (c + 1) * n], axes, axis=0, tiled=False)
-        dq, dkv = attend_call(c, n, group, queries, out_grad, kv_all)
+        flat = kv[c * n : (c + 1) * n].reshape(n * 2 * local_slots, width)
+        own = lax.all_gather(flat, "seq", axis=0, tiled=False)
+        other = lax.ppermute(own, "dp", swap)
+        ranks = own.shape[0]
+        dq, down, dother = attend_call(
+            c, n, group, queries, out_grad, own.reshape((ranks,) + block), other.reshape((ranks,) + block)
+        )
         query_grads.append(dq)
-        shares.append(lax.psum_scatter(dkv, axes, scatter_dimension=0, tiled=False))
+        flat_grad = (ranks, n * 2 * local_slots, width)
+        arrived = lax.ppermute(dother.reshape(flat_grad), "dp", swap)
+        pair = (down.reshape(flat_grad) + arrived).astype(jnp.bfloat16)
+        share = lax.psum_scatter(pair, "seq", scatter_dimension=0, tiled=False)
+        shares.append(share.astype(jnp.float32).reshape(block))
     query_grad = jnp.concatenate(query_grads, axis=1)
     share = jnp.concatenate(shares, axis=0).transpose(1, 2, 0, 3)
     return (query_grad, share[0] * key_pass, share[1] * value_pass)

time: 499 us -> 456 us (0.914)
  waiting for transfers between devices: 350 us -> 308 us
  local copies, waits for them, and re-layouts: 17.2 us -> 5.06 us
  other arithmetic: 9.43 us -> 18.2 us
    reduce_scatter x4, waiting for transfers between devices: 268 us -> 195 us  [local(): share = lax.psum_scatter(pair, 'seq', scatter_dimension=0, tiled=False)]
    all_gather x4, waiting for transfers between devices: 79.6 us -> 106 us  [local(): own = lax.all_gather(flat, 'seq', axis=0, tiled=False)]
    all_gather x4 -> x0, local copies, waits for them, and re-layouts: 12.6 us -> none  [local(): kv_all = lax.all_gather(kv[c * n:(c + 1) * n], axes, axis=0, tiled=False)]
    convert_element_type x0 -> x4, other arithmetic: none -> 8.8 us  [local(): pair = (down.reshape(flat_grad) + arrived).astype(jnp.bfloat16)]
    ppermute x0 -> x8, waiting for transfers between devices: none -> 6.01 us  [the longest x4 3.21 us: local(): arrived = lax.ppermute(dother.reshape(flat_grad), 'dp', swap)]
  transfers between devices with their start and end apart: 8 -> 16, of which waited for: 8 -> 9; matrix products, arithmetic and copies ran while one was open for 3% -> 2% of each run, Pallas kernels for 21% -> 24%
where the time goes in v2:
time: 456 us; the launch traced here: 455 us
  waiting for transfers between devices  308 us (68%)
  Pallas kernels  108 us (24%)
  other arithmetic  18.2 us (4%)
  between operations  14.3 us (3%)
  local copies, waits for them, and re-layouts  5.06 us (1%)
    reduce_scatter x4, waiting for transfers between devices, local(): share = lax.psum_scatter(pair, 'seq', scatter_dimension=0, tiled=False)  195 us
    pallas_call x4, Pallas kernels, attend_call(): pl.pallas_call(functools.partial(attend_kernel, heads, group), grid=(toke...  108 us
    all_gather x4, waiting for transfers between devices, local(): own = lax.all_gather(flat, 'seq', axis=0, tiled=False)  106 us
  transfers between devices with their start and end apart: 16, of which 9 were waited for; matrix products, arithmetic and copies ran while one was open for 2% of the time, Pallas kernels for 24%

profile of v2, /device:TPU:0, one launch (start us, length us, event | category | flops | bytes accessed | tf_op | source)
XLA Modules:
  0.0 455.3 jit_solution(24602533499983969)
XLA Ops:
  7.2 0.0 all-gather.5.cloned.1.call-start
  7.2 0.8 fusion.28
  8.0 3.1 compare_reduce_fusion
  11.1 0.1 copy.38
  11.2 1.9 fusion.12
  13.1 0.1 maximum_bitcast_fusion
  13.2 0.8 fusion.74
  14.0 0.0 all-gather.5.cloned.1.call-update
  14.0 0.0 all-gather.7.cloned.1.call-start
  14.0 0.7 all-gather.7.cloned.1.call-update
  14.7 0.0 all-gather.9.cloned.1.call-start
  14.8 42.2 %all-gather.5.cloned.1.call-done = bf16[8,512,128]{2,1,0:T(8,128)(2,1)} async-done(((bf16[1,512,128]{2,1,0:T(8,128)(2,1)}), bf16[8,512,128]{2,1,0:T(8,128)(2,1)}) %all-gather.5.cloned.1.call-update) | async-done | bytes 1048592 | tf_op jit(solution)/shard_map/all_gather | solution.py:142
  57.0 0.0 collective-permute-start
  57.0 0.0 all-gather.9.cloned.1.call-update
  57.0 0.0 all-gather.11.cloned.1.call-start
  57.1 2.8 collective-permute-done
  59.9 1.0 copy-done.10
  60.8 26.8 %shard_map.85 = (bf16[128,16,128]{2,1,0:T(8,128)(2,1)}, f32[8,2,2,128,128]{4,3,2,1,0:T(8,128)}, f32[8,2,2,128,128]{4,3,2,1,0:T(8,128)}) custom-call(bf16[128,64,128]{2,1,0:T(8,128)(2,1)} %q_ref.7, bf16[128,64,128]{2,1,0:T(8,128)(2,1)} %g_ref.7, bf16[8,2,2,128,128]{4,3,2,1,0:T(8,128)(2,1)} %bitcast.94, bf16[8,2,2,128,128]{4,3,2,1,0:T(8,128)(2,1)} %bitcast.95), custom_call_target="tpu_custom_call" | custom-call | flops 10737418240 | bytes 12582912 | tf_op jit(solution)/shard_map/pallas_call | solution.py:100
  87.6 0.1 collective-permute-start.4
  87.8 10.3 %all-gather.7.cloned.1.call-done = bf16[8,512,128]{2,1,0:T(8,128)(2,1)} async-done(((bf16[1,512,128]{2,1,0:T(8,128)(2,1)}), bf16[8,512,128]{2,1,0:T(8,128)(2,1)}) %all-gather.7.cloned.1.call-update) | async-done | bytes 1048592 | tf_op jit(solution)/shard_map/all_gather | solution.py:142
  98.1 0.0 collective-permute-start.1
  98.1 0.0 all-gather.11.cloned.1.call-update
  98.1 0.2 reduce-scatter.5.cloned.1.call-start
  98.3 40.8 %all-gather.9.cloned.1.call-done = bf16[8,512,128]{2,1,0:T(8,128)(2,1)} async-done(((bf16[1,512,128]{2,1,0:T(8,128)(2,1)}), bf16[8,512,128]{2,1,0:T(8,128)(2,1)}) %all-gather.9.cloned.1.call-update) | async-done | bytes 1048592 | tf_op jit(solution)/shard_map/all_gather | solution.py:142
  139.2 0.0 collective-permute-start.2
  139.2 0.0 collective-permute-done.1
  139.2 26.9 %shard_map.86 = (bf16[128,16,128]{2,1,0:T(8,128)(2,1)}, f32[8,2,2,128,128]{4,3,2,1,0:T(8,128)}, f32[8,2,2,128,128]{4,3,2,1,0:T(8,128)}) custom-call(bf16[128,64,128]{2,1,0:T(8,128)(2,1)} %q_ref.7, bf16[128,64,128]{2,1,0:T(8,128)(2,1)} %g_ref.7, bf16[8,2,2,128,128]{4,3,2,1,0:T(8,128)(2,1)} %bitcast.92, bf16[8,2,2,128,128]{4,3,2,1,0:T(8,128)(2,1)} %bitcast.16.other_ref), custom_call_target="tpu_custom_call" | custom-call | flops 10737418240 | bytes 12582912 | tf_op jit(solution)/shard_map/pallas_call | solution.py:100
  166.1 0.5 collective-permute-start.5
  166.6 0.0 collective-permute-done.4
  166.6 1.2 fusion.3
  167.9 0.0 reduce-scatter.5.cloned.1.call-update
  167.9 0.3 reduce-scatter.7.cloned.1.call-start
  168.1 12.6 %all-gather.11.cloned.1.call-done = bf16[8,512,128]{2,1,0:T(8,128)(2,1)} async-done(((bf16[1,512,128]{2,1,0:T(8,128)(2,1)}), bf16[8,512,128]{2,1,0:T(8,128)(2,1)}) %all-gather.11.cloned.1.call-update) | async-done | bytes 1048592 | tf_op jit(solution)/shard_map/all_gather | solution.py:142
  180.8 0.0 collective-permute-start.3
  180.8 0.0 collective-permute-done.2
  180.8 1.0 copy-done.9
  181.8 27.0 %shard_map.87 = (bf16[128,16,128]{2,1,0:T(8,128)(2,1)}, f32[8,2,2,128,128]{4,3,2,1,0:T(8,128)}, f32[8,2,2,128,128]{4,3,2,1,0:T(8,128)}) custom-call(bf16[128,64,128]{2,1,0:T(8,128)(2,1)} %q_ref.7, bf16[128,64,128]{2,1,0:T(8,128)(2,1)} %g_ref.7, bf16[8,2,2,128,128]{4,3,2,1,0:T(8,128)(2,1)} %bitcast.90, bf16[8,2,2,128,128]{4,3,2,1,0:T(8,128)(2,1)} %bitcast.93), custom_call_target="tpu_custom_call" | custom-call | flops 10737418240 | bytes 12582912 | tf_op jit(solution)/shard_map/pallas_call | solution.py:100
  208.7 0.5 collective-permute-start.6
  209.2 0.0 collective-permute-done.5
  209.2 0.0 copy-done.1
  209.2 2.8 fusion.2
  212.1 0.0 reduce-scatter.7.cloned.1.call-update
  212.1 0.3 reduce-scatter.9.cloned.1.call-start
  212.4 0.0 collective-permute-done.3
  212.4 27.0 %shard_map.88 = (bf16[128,16,128]{2,1,0:T(8,128)(2,1)}, f32[8,2,2,128,128]{4,3,2,1,0:T(8,128)}, f32[8,2,2,128,128]{4,3,2,1,0:T(8,128)}) custom-call(bf16[128,64,128]{2,1,0:T(8,128)(2,1)} %q_ref.7, bf16[128,64,128]{2,1,0:T(8,128)(2,1)} %g_ref.7, bf16[8,2,2,128,128]{4,3,2,1,0:T(8,128)(2,1)} %bitcast.91, bf16[8,2,2,128,128]{4,3,2,1,0:T(8,128)(2,1)} %bitcast.22.other_ref), custom_call_target="tpu_custom_call" | custom-call | flops 10737418240 | bytes 12582912 | tf_op jit(solution)/shard_map/pallas_call | solution.py:100
  239.4 0.0 collective-permute-start.7
  239.4 0.0 collective-permute-done.6
  239.4 1.2 fusion.1
  240.6 0.0 reduce-scatter.9.cloned.1.call-update
  240.6 0.0 reduce-scatter.11.cloned.1.call-start
  240.7 3.2 collective-permute-done.7
  243.9 3.6 fusion
  247.5 0.0 reduce-scatter.11.cloned.1.call-update
  247.6 0.0 copy-start.3
  247.6 0.0 copy-start.4
  247.6 1.6 pad_maximum_fusion
  249.2 63.0 %reduce-scatter.7.cloned.1.call-done = bf16[1,512,128]{2,1,0:T(8,128)(2,1)} async-done(((bf16[8,512,128]{2,1,0:T(8,128)(2,1)}), bf16[1,512,128]{2,1,0:T(8,128)(2,1)}) %reduce-scatter.7.cloned.1.call-update) | async-done | bytes 131088 | tf_op jit(solution)/shard_map/reduce_scatter | solution.py:152
  312.2 65.8 %reduce-scatter.9.cloned.1.call-done = bf16[1,512,128]{2,1,0:T(8,128)(2,1)} async-done(((bf16[8,512,128]{2,1,0:T(8,128)(2,1)}), bf16[1,512,128]{2,1,0:T(8,128)(2,1)}) %reduce-scatter.9.cloned.1.call-update) | async-done | bytes 131088 | tf_op jit(solution)/shard_map/reduce_scatter | solution.py:152
  378.0 66.2 %reduce-scatter.11.cloned.1.call-done = bf16[1,512,128]{2,1,0:T(8,128)(2,1)} async-done(((bf16[8,512,128]{2,1,0:T(8,128)(2,1)}), bf16[1,512,128]{2,1,0:T(8,128)(2,1)}) %reduce-scatter.11.cloned.1.call-update) | async-done | bytes 131088 | tf_op jit(solution)/shard_map/reduce_scatter | solution.py:152
  444.3 1.2 convert_bitcast_fusion
  445.5 0.0 copy-done.3
  445.5 0.7 fusion.4
  446.2 1.1 copy.48
  447.3 1.1 copy.49
  (20 shorter events, 0.1 us)
Async XLA Ops:
  7.2 49.8 %all-gather.5.cloned.1.call-start = ((), (), s32[]{:S(2)}) async-start(), calls=%async_computation.4 | async-start | bytes 1179648 | tf_op jit(solution)/shard_map/all_gather | solution.py:142
  14.0 84.1 %all-gather.7.cloned.1.call-start = ((), (), s32[]{:S(2)}) async-start(), calls=%async_computation.5 | async-start | bytes 1179648 | tf_op jit(solution)/shard_map/all_gather | solution.py:142
  14.7 124.4 %all-gather.9.cloned.1.call-start = ((), (), s32[]{:S(2)}) async-start(), calls=%async_computation.6 | async-start | bytes 1179648 | tf_op jit(solution)/shard_map/all_gather | solution.py:142
  57.0 2.9 collective-permute-start
  57.0 123.7 %all-gather.11.cloned.1.call-start = ((), (), s32[]{:S(2)}) async-start(), calls=%async_computation.7 | async-start | bytes 1179648 | tf_op jit(solution)/shard_map/all_gather | solution.py:142
  59.9 1.0 copy-start.10
  87.6 79.0 %collective-permute-start.4 = (f32[8,512,128]{2,1,0:T(8,128)}, f32[8,512,128]{2,1,0:T(8,128)S(1)}, u32[]{:S(2)}, u32[]{:S(2)}) collective-permute-start(f32[8,512,128]{2,1,0:T(8,128)} %bitcast.86), channel_id=1, source_target_pairs={{0,8},{8,0},{1,9},{9,1},{2,10},{10,2},{3,11},{11,3},{4,12},{12,4},... | collective-permute-start | bytes 6291464 | tf_op jit(solution)/shard_map/ppermute | solution.py:150
  98.1 41.1 %collective-permute-start.1 = (bf16[8,512,128]{2,1,0:T(8,128)(2,1)}, bf16[8,512,128]{2,1,0:T(8,128)(2,1)}, u32[]{:S(2)}, u32[]{:S(2)}) collective-permute-start(bf16[8,512,128]{2,1,0:T(8,128)(2,1)} %all-gather.7.cloned.1.call-done), channel_id=1, source_target_pairs={{0,8},{8,0},{1,9},{9,1},{2,10},{10,2},{3,11},{11,3},{4,12},{12,4},... | collective-permute-start | bytes 3145736 | tf_op jit(solution)/shard_map/ppermute | solution.py:143
  98.1 151.1 %reduce-scatter.5.cloned.1.call-start = ((), (), s32[]{:S(2)}) async-start(), calls=%async_computation.8 | async-start | bytes 1179648 | tf_op jit(solution)/shard_map/reduce_scatter | solution.py:152
  139.2 41.6 %collective-permute-start.2 = (bf16[8,512,128]{2,1,0:T(8,128)(2,1)}, bf16[8,512,128]{2,1,0:T(8,128)(2,1)S(1)}, u32[]{:S(2)}, u32[]{:S(2)}) collective-permute-start(bf16[8,512,128]{2,1,0:T(8,128)(2,1)} %all-gather.9.cloned.1.call-done), channel_id=1, source_target_pairs={{0,8},{8,0},{1,9},{9,1},{2,10},{10,2},{3,11},{11,3},{4,12},{12,4},... | collective-permute-start | bytes 3145736 | tf_op jit(solution)/shard_map/ppermute | solution.py:143
  139.2 27.5 %copy-start = (f32[8,2,2,128,128]{4,3,2,1,0:T(8,128)S(1)}, f32[8,2,2,128,128]{4,3,2,1,0:T(8,128)}, u32[]{:S(2)}) copy-start(f32[8,2,2,128,128]{4,3,2,1,0:T(8,128)} %get-tuple-element.19) | copy-start | bytes 6291460
  166.1 43.1 %collective-permute-start.5 = (f32[8,512,128]{2,1,0:T(8,128)}, f32[8,512,128]{2,1,0:T(8,128)}, u32[]{:S(2)}, u32[]{:S(2)}) collective-permute-start(f32[8,512,128]{2,1,0:T(8,128)} %bitcast.87), channel_id=1, source_target_pairs={{0,8},{8,0},{1,9},{9,1},{2,10},{10,2},{3,11},{11,3},{4,12},{12,4},... | collective-permute-start | bytes 6291464 | tf_op jit(solution)/shard_map/ppermute | solution.py:150
  167.9 144.3 %reduce-scatter.7.cloned.1.call-start = ((), (), s32[]{:S(2)}) async-start(), calls=%async_computation.9 | async-start | bytes 1179648 | tf_op jit(solution)/shard_map/reduce_scatter | solution.py:152
  180.8 31.6 %collective-permute-start.3 = (bf16[8,512,128]{2,1,0:T(8,128)(2,1)}, bf16[8,512,128]{2,1,0:T(8,128)(2,1)}, u32[]{:S(2)}, u32[]{:S(2)}) collective-permute-start(bf16[8,512,128]{2,1,0:T(8,128)(2,1)} %all-gather.11.cloned.1.call-done), channel_id=1, source_target_pairs={{0,8},{8,0},{1,9},{9,1},{2,10},{10,2},{3,11},{11,3},{4,12},{12,4},... | collective-permute-start | bytes 3145736 | tf_op jit(solution)/shard_map/ppermute | solution.py:143
  180.8 1.0 copy-start.9
  181.8 27.5 %copy-start.1 = (f32[8,2,2,128,128]{4,3,2,1,0:T(8,128)S(1)}, f32[8,2,2,128,128]{4,3,2,1,0:T(8,128)}, u32[]{:S(2)}) copy-start(f32[8,2,2,128,128]{4,3,2,1,0:T(8,128)} %get-tuple-element.21) | copy-start | bytes 6291460
  208.7 30.7 %collective-permute-start.6 = (f32[8,512,128]{2,1,0:T(8,128)}, f32[8,512,128]{2,1,0:T(8,128)S(1)}, u32[]{:S(2)}, u32[]{:S(2)}) collective-permute-start(f32[8,512,128]{2,1,0:T(8,128)} %bitcast.88), channel_id=1, source_target_pairs={{0,8},{8,0},{1,9},{9,1},{2,10},{10,2},{3,11},{11,3},{4,12},{12,4},... | collective-permute-start | bytes 6291464 | tf_op jit(solution)/shard_map/ppermute | solution.py:150
  212.1 166.0 %reduce-scatter.9.cloned.1.call-start = ((), (), s32[]{:S(2)}) async-start(), calls=%async_computation.10 | async-start | bytes 1179648 | tf_op jit(solution)/shard_map/reduce_scatter | solution.py:152
  212.4 27.0 %copy-start.2 = (f32[8,2,2,128,128]{4,3,2,1,0:T(8,128)S(1)}, f32[8,2,2,128,128]{4,3,2,1,0:T(8,128)}, u32[]{:S(2)}) copy-start(f32[8,2,2,128,128]{4,3,2,1,0:T(8,128)} %get-tuple-element.23) | copy-start | bytes 6291460
  239.4 4.5 collective-permute-start.7
  240.6 203.6 %reduce-scatter.11.cloned.1.call-start = ((), (), s32[]{:S(2)}) async-start(), calls=%async_computation.11 | async-start | bytes 1179648 | tf_op jit(solution)/shard_map/reduce_scatter | solution.py:152
  243.9 3.6 copy-start.5
  243.9 3.6 copy-start.6
  243.9 3.6 copy-start.7
  243.9 3.6 copy-start.8
  247.6 197.9 %copy-start.3 = (f32[128,8,128]{2,1,0:T(8,128)S(1)}, f32[128,8,128]{2,1,0:T(8,128)}, u32[]{:S(2)}) copy-start(f32[128,8,128]{2,1,0:T(8,128)} %param.8) | copy-start | bytes 1572868
  247.6 197.9 %copy-start.4 = (f32[128,8,128]{2,1,0:T(8,128)S(1)}, f32[128,8,128]{2,1,0:T(8,128)}, u32[]{:S(2)}) copy-start(f32[128,8,128]{2,1,0:T(8,128)} %param.9) | copy-start | bytes 1572868
Sparse Core Ops, SparseCore 0:
  14.1 42.8 all-gather.4
  59.1 38.9 all-gather.6
  100.2 38.8 all-gather.8
  141.7 38.9 all-gather.10
  184.0 62.1 reduce-scatter.4
  249.8 62.3 reduce-scatter.6
  315.6 62.3 reduce-scatter.8
  381.8 62.4 reduce-scatter.10

commit v3 on v2

--- a/solution.py
+++ b/solution.py
@@ -9,7 +9,8 @@
 from jax.sharding import PartitionSpec as P
 
 TOKEN_BLOCK = 32
-HEADS_PER_CALL = 2
+HEADS_PER_CALL = 4
+HEADS_PER_STEP = 2
 
 
 def step_tables(exponent):
@@ -51,7 +52,7 @@
     to_exp2 = inv_root * math.log2(math.e)
     q_all = q_ref[...].astype(jnp.float32)
     g_all = g_ref[...].astype(jnp.float32)
-    first = pl.program_id(0) == 0
+    first = pl.program_id(1) == 0
     outs = []
     for h in range(heads):
         q = q_all[:, h * group : (h + 1) * group].reshape(rows, width).astype(jnp.bfloat16)
@@ -96,20 +97,24 @@
     devices, _, _, part, _ = own.shape
     tb = math.gcd(tokens, TOKEN_BLOCK)
     wide = heads * group
+    step = math.gcd(heads, HEADS_PER_STEP)
+    pairs = heads // step
+    rows = (tb, step * group, width)
+    block = (devices, step, 2, part, width)
     flops = 20 * tokens * wide * devices * part * width
     return pl.pallas_call(
-        functools.partial(attend_kernel, heads, group),
-        grid=(tokens // tb,),
+        functools.partial(attend_kernel, step, group),
+        grid=(pairs, tokens // tb),
         in_specs=[
-            pl.BlockSpec((tb, wide, width), lambda i: (i, index, 0)),
-            pl.BlockSpec((tb, wide, width), lambda i: (i, index, 0)),
-            pl.BlockSpec(own.shape, lambda i: (0, 0, 0, 0, 0)),
-            pl.BlockSpec(own.shape, lambda i: (0, 0, 0, 0, 0)),
+            pl.BlockSpec(rows, lambda j, i: (i, index * pairs + j, 0)),
+            pl.BlockSpec(rows, lambda j, i: (i, index * pairs + j, 0)),
+            pl.BlockSpec(block, lambda j, i: (0, j, 0, 0, 0)),
+            pl.BlockSpec(block, lambda j, i: (0, j, 0, 0, 0)),
         ],
         out_specs=[
-            pl.BlockSpec((tb, wide, width), lambda i: (i, 0, 0)),
-            pl.BlockSpec(own.shape, lambda i: (0, 0, 0, 0, 0)),
-            pl.BlockSpec(own.shape, lambda i: (0, 0, 0, 0, 0)),
+            pl.BlockSpec(rows, lambda j, i: (i, j, 0)),
+            pl.BlockSpec(block, lambda j, i: (0, j, 0, 0, 0)),
+            pl.BlockSpec(block, lambda j, i: (0, j, 0, 0, 0)),
         ],
         out_shape=[
             jax.ShapeDtypeStruct((tokens, wide, width), jnp.bfloat16),

time: 456 us -> 336 us (0.74)
  waiting for transfers between devices: 308 us -> 195 us
  Pallas kernels: 108 us -> 101 us
    reduce_scatter x4 -> x2, waiting for transfers between devices: 195 us -> 126 us  [local(): share = lax.psum_scatter(pair, 'seq', scatter_dimension=0, tiled=False)]
    all_gather x4 -> x2, waiting for transfers between devices: 106 us -> 52.1 us  [local(): own = lax.all_gather(flat, 'seq', axis=0, tiled=False)]
    ppermute x4 -> x2, waiting for transfers between devices: 2.8 us -> 13.7 us  [local(): other = lax.ppermute(own, 'dp', swap)]
    pallas_call x4 -> x2, Pallas kernels: 108 us -> 101 us  [attend_call(): pl.pallas_call(functools.partial(attend_kernel, step, group), grid=(pairs...]
    convert_element_type x4 -> x2, other arithmetic: 8.8 us -> 9.53 us  [local(): pair = (down.reshape(flat_grad) + arrived).astype(jnp.bfloat16)]
  transfers between devices with their start and end apart: 16 -> 8, of which waited for: 9 -> 6; matrix products, arithmetic and copies ran while one was open for 2% -> 3% of each run, Pallas kernels for 24% -> 30%
where the time goes in v3:
time: 336 us
  waiting for transfers between devices  195 us (58%)
  Pallas kernels  101 us (30%)
  other arithmetic  18.9 us (6%)
  between operations  13.9 us (4%)
  local copies, waits for them, and re-layouts  5.75 us (2%)
    reduce_scatter x2, waiting for transfers between devices, local(): share = lax.psum_scatter(pair, 'seq', scatter_dimension=0, tiled=False)  126 us
    pallas_call x2, Pallas kernels, attend_call(): pl.pallas_call(functools.partial(attend_kernel, step, group), grid=(pairs...  101 us
    all_gather x2, waiting for transfers between devices, local(): own = lax.all_gather(flat, 'seq', axis=0, tiled=False)  52.1 us
    ppermute x2, waiting for transfers between devices, local(): other = lax.ppermute(own, 'dp', swap)  13.7 us
    convert_element_type x2, other arithmetic, local(): pair = (down.reshape(flat_grad) + arrived).astype(jnp.bfloat16)  9.53 us
  transfers between devices with their start and end apart: 8, of which 6 were waited for; matrix products, arithmetic and copies ran while one was open for 3% of the time, Pallas kernels for 30%

profile of v3, /device:TPU:0, one launch (start us, length us, event | category | flops | bytes accessed | tf_op | source)
XLA Modules:
  0.0 335.8 jit_solution(9714676476066858284)
XLA Ops:
  7.2 0.0 all-gather.3.cloned.1.call-start
  7.2 0.8 fusion.26
  8.0 3.1 compare_reduce_fusion
  11.1 0.1 copy.34
  11.2 1.9 fusion.10
  13.1 0.1 maximum_bitcast_fusion
  13.2 0.8 fusion.72
  14.0 0.0 all-gather.3.cloned.1.call-update
  14.0 0.0 all-gather.5.cloned.1.call-start
  14.1 52.1 %all-gather.3.cloned.1.call-done = bf16[8,1024,128]{2,1,0:T(8,128)(2,1)} async-done(((bf16[1,1024,128]{2,1,0:T(8,128)(2,1)}), bf16[8,1024,128]{2,1,0:T(8,128)(2,1)}) %all-gather.3.cloned.1.call-update) | async-done | bytes 2097168 | tf_op jit(solution)/shard_map/all_gather | solution.py:147
  66.2 0.0 collective-permute-start
  66.2 0.0 all-gather.5.cloned.1.call-update
  66.2 0.2 reduce-scatter.3.cloned.1.call-start
  66.4 4.1 %collective-permute-done = bf16[8,1024,128]{2,1,0:T(8,128)(2,1)S(1)} collective-permute-done((bf16[8,1024,128]{2,1,0:T(8,128)(2,1)}, bf16[8,1024,128]{2,1,0:T(8,128)(2,1)S(1)}, u32[]{:S(2)}, u32[]{:S(2)}) %collective-permute-start) | collective-permute-done | bytes 2097184 | tf_op jit(solution)/shard_map/ppermute | solution.py:148
  70.5 0.0 copy-start.5
  70.5 1.3 copy-done.5
  71.9 50.3 %shard_map.85 = (bf16[128,32,128]{2,1,0:T(8,128)(2,1)}, f32[8,4,2,128,128]{4,3,2,1,0:T(8,128)}, f32[8,4,2,128,128]{4,3,2,1,0:T(8,128)}) custom-call(bf16[128,64,128]{2,1,0:T(8,128)(2,1)} %q_ref.3, bf16[128,64,128]{2,1,0:T(8,128)(2,1)} %g_ref.3, bf16[8,4,2,128,128]{4,3,2,1,0:T(8,128)(2,1)} %bitcast.67, bf16[8,4,2,128,128]{4,3,2,1,0:T(8,128)(2,1)} %bitcast.68), custom_call_target="tpu_custom_call" | custom-call | flops 21474836480 | bytes 12582912 | tf_op jit(solution)/shard_map/pallas_call | solution.py:105
  122.2 0.1 collective-permute-start.2
  122.3 0.0 all-gather.5.cloned.1.call-done
  122.3 0.4 collective-permute-start.1
  122.7 9.6 %collective-permute-done.1 = bf16[8,1024,128]{2,1,0:T(8,128)(2,1)S(1)} collective-permute-done((bf16[8,1024,128]{2,1,0:T(8,128)(2,1)}, bf16[8,1024,128]{2,1,0:T(8,128)(2,1)S(1)}, u32[]{:S(2)}, u32[]{:S(2)}) %collective-permute-start.1) | collective-permute-done | bytes 2097184 | tf_op jit(solution)/shard_map/ppermute | solution.py:148
  132.3 0.0 copy-start.6
  132.3 1.3 copy-done.6
  133.6 0.0 copy-start
  133.6 50.5 %shard_map.86 = (bf16[128,32,128]{2,1,0:T(8,128)(2,1)}, f32[8,4,2,128,128]{4,3,2,1,0:T(8,128)}, f32[8,4,2,128,128]{4,3,2,1,0:T(8,128)}) custom-call(bf16[128,64,128]{2,1,0:T(8,128)(2,1)} %q_ref.3, bf16[128,64,128]{2,1,0:T(8,128)(2,1)} %g_ref.3, bf16[8,4,2,128,128]{4,3,2,1,0:T(8,128)(2,1)} %bitcast.66, bf16[8,4,2,128,128]{4,3,2,1,0:T(8,128)(2,1)} %bitcast.69), custom_call_target="tpu_custom_call" | custom-call | flops 21474836480 | bytes 12582912 | tf_op jit(solution)/shard_map/pallas_call | solution.py:105
  184.1 0.4 collective-permute-start.3
  184.4 0.0 collective-permute-done.2
  184.4 0.0 copy-done
  184.4 4.0 %fusion.1 = bf16[8,1024,128]{2,1,0:T(8,128)(2,1)} fusion(f32[8,1024,128]{2,1,0:T(8,128)} %collective-permute-done.2, f32[8,4,2,128,128]{4,3,2,1,0:T(8,128)S(1)} %copy-done), kind=kLoop, calls=%fused_computation.3 | loop fusion | flops 2097152 | bytes 10485760 | tf_op jit(solution)/shard_map/convert_element_type | solution.py:156
  188.4 0.0 reduce-scatter.3.cloned.1.call-update
  188.4 0.0 reduce-scatter.5.cloned.1.call-start
  188.5 3.1 collective-permute-done.3
  191.6 0.0 copy-start.3
  191.6 0.0 copy-start.4
  191.6 5.5 %fusion = bf16[8,1024,128]{2,1,0:T(8,128)(2,1)} fusion(f32[8,1024,128]{2,1,0:T(8,128)} %collective-permute-done.3, f32[8,4,2,128,128]{4,3,2,1,0:T(8,128)} %get-tuple-element.13), kind=kLoop, calls=%fused_computation.1 | loop fusion | flops 2097152 | bytes 10485760 | tf_op jit(solution)/shard_map/convert_element_type | solution.py:156
  197.1 0.0 copy-start.1
  197.1 0.0 copy-start.2
  197.1 0.0 reduce-scatter.5.cloned.1.call-update
  197.1 0.0 copy-done.3
  197.2 0.0 copy-done.4
  197.2 1.6 pad_maximum_fusion
  198.8 56.2 %reduce-scatter.3.cloned.1.call-done = bf16[1,1024,128]{2,1,0:T(8,128)(2,1)} async-done(((bf16[8,1024,128]{2,1,0:T(8,128)(2,1)}), bf16[1,1024,128]{2,1,0:T(8,128)(2,1)}) %reduce-scatter.3.cloned.1.call-update) | async-done | bytes 262160 | tf_op jit(solution)/shard_map/reduce_scatter | solution.py:157
  255.0 70.2 %reduce-scatter.5.cloned.1.call-done = bf16[1,1024,128]{2,1,0:T(8,128)(2,1)} async-done(((bf16[8,1024,128]{2,1,0:T(8,128)(2,1)}), bf16[1,1024,128]{2,1,0:T(8,128)(2,1)}) %reduce-scatter.5.cloned.1.call-update) | async-done | bytes 262160 | tf_op jit(solution)/shard_map/reduce_scatter | solution.py:157
  325.2 1.1 convert_bitcast_fusion
  326.3 0.0 copy-done.1
  326.3 0.0 copy-done.2
  326.3 0.7 fusion.2
  327.0 1.1 copy.42
  328.1 1.1 copy.43
  (3 shorter events, 0.1 us)
Async XLA Ops:
  7.2 59.0 %all-gather.3.cloned.1.call-start = ((), (), s32[]{:S(2)}) async-start(), calls=%async_computation.2 | async-start | bytes 2359296 | tf_op jit(solution)/shard_map/all_gather | solution.py:147
  14.0 108.3 %all-gather.5.cloned.1.call-start = ((), (), s32[]{:S(2)}) async-start(), calls=%async_computation.3 | async-start | bytes 2359296 | tf_op jit(solution)/shard_map/all_gather | solution.py:147
  66.2 4.4 %collective-permute-start = (bf16[8,1024,128]{2,1,0:T(8,128)(2,1)}, bf16[8,1024,128]{2,1,0:T(8,128)(2,1)S(1)}, u32[]{:S(2)}, u32[]{:S(2)}) collective-permute-start(bf16[8,1024,128]{2,1,0:T(8,128)(2,1)} %all-gather.3.cloned.1.call-done), channel_id=1, source_target_pairs={{0,8},{8,0},{1,9},{9,1},{2,10},{10,2},{3,11},{11,3},{4,12},{12,4},... | collective-permute-start | bytes 6291464 | tf_op jit(solution)/shard_map/ppermute | solution.py:148
  66.2 188.8 %reduce-scatter.3.cloned.1.call-start = ((), (), s32[]{:S(2)}) async-start(), calls=%async_computation.4 | async-start | bytes 2359296 | tf_op jit(solution)/shard_map/reduce_scatter | solution.py:157
  70.5 1.3 copy-start.5
  122.2 62.3 %collective-permute-start.2 = (f32[8,1024,128]{2,1,0:T(8,128)}, f32[8,1024,128]{2,1,0:T(8,128)}, u32[]{:S(2)}, u32[]{:S(2)}) collective-permute-start(f32[8,1024,128]{2,1,0:T(8,128)} %bitcast.64), channel_id=1, source_target_pairs={{0,8},{8,0},{1,9},{9,1},{2,10},{10,2},{3,11},{11,3},{4,12},{12,4},... | collective-permute-start | bytes 12582920 | tf_op jit(solution)/shard_map/ppermute | solution.py:155
  122.3 10.0 %collective-permute-start.1 = (bf16[8,1024,128]{2,1,0:T(8,128)(2,1)}, bf16[8,1024,128]{2,1,0:T(8,128)(2,1)S(1)}, u32[]{:S(2)}, u32[]{:S(2)}) collective-permute-start(bf16[8,1024,128]{2,1,0:T(8,128)(2,1)} %all-gather.5.cloned.1.call-done), channel_id=1, source_target_pairs={{0,8},{8,0},{1,9},{9,1},{2,10},{10,2},{3,11},{11,3},{4,12},{12,4},... | collective-permute-start | bytes 6291464 | tf_op jit(solution)/shard_map/ppermute | solution.py:148
  132.3 1.3 copy-start.6
  133.6 50.8 %copy-start = (f32[8,4,2,128,128]{4,3,2,1,0:T(8,128)S(1)}, f32[8,4,2,128,128]{4,3,2,1,0:T(8,128)}, u32[]{:S(2)}) copy-start(f32[8,4,2,128,128]{4,3,2,1,0:T(8,128)} %get-tuple-element.11) | copy-start | bytes 12582916
  184.1 7.5 %collective-permute-start.3 = (f32[8,1024,128]{2,1,0:T(8,128)}, f32[8,1024,128]{2,1,0:T(8,128)}, u32[]{:S(2)}, u32[]{:S(2)}) collective-permute-start(f32[8,1024,128]{2,1,0:T(8,128)} %bitcast.65), channel_id=1, source_target_pairs={{0,8},{8,0},{1,9},{9,1},{2,10},{10,2},{3,11},{11,3},{4,12},{12,4},... | collective-permute-start | bytes 12582920 | tf_op jit(solution)/shard_map/ppermute | solution.py:155
  188.4 136.7 %reduce-scatter.5.cloned.1.call-start = ((), (), s32[]{:S(2)}) async-start(), calls=%async_computation.5 | async-start | bytes 2359296 | tf_op jit(solution)/shard_map/reduce_scatter | solution.py:157
  191.6 5.6 %copy-start.3 = (bf16[128,32,128]{2,1,0:T(8,128)(2,1)S(1)}, bf16[128,32,128]{2,1,0:T(8,128)(2,1)}, u32[]{:S(2)}) copy-start(bf16[128,32,128]{2,1,0:T(8,128)(2,1)} %get-tuple-element.9) | copy-start | bytes 3145732
  191.6 5.6 %copy-start.4 = (bf16[128,32,128]{2,1,0:T(8,128)(2,1)S(1)}, bf16[128,32,128]{2,1,0:T(8,128)(2,1)}, u32[]{:S(2)}) copy-start(bf16[128,32,128]{2,1,0:T(8,128)(2,1)} %get-tuple-element.10) | copy-start | bytes 3145732
  197.1 129.2 %copy-start.1 = (f32[128,8,128]{2,1,0:T(8,128)S(1)}, f32[128,8,128]{2,1,0:T(8,128)}, u32[]{:S(2)}) copy-start(f32[128,8,128]{2,1,0:T(8,128)} %param.8) | copy-start | bytes 1572868
  197.1 129.2 %copy-start.2 = (f32[128,8,128]{2,1,0:T(8,128)S(1)}, f32[128,8,128]{2,1,0:T(8,128)}, u32[]{:S(2)}) copy-start(f32[128,8,128]{2,1,0:T(8,128)} %param.9) | copy-start | bytes 1572868
Sparse Core Ops, SparseCore 0:
  14.2 51.9 all-gather.2
  68.9 47.8 all-gather.4
  188.6 66.3 reduce-scatter.2
  258.4 66.7 reduce-scatter.4

commit v4 on v3

--- a/solution.py
+++ b/solution.py
@@ -139,7 +139,7 @@
     value_used, value_pass = fake_quant(cache_values, exponents[:, 1, :], marked)
     kv = jnp.stack([key_used, value_used], axis=0).transpose(2, 0, 1, 3)
     n = HEADS_PER_CALL
-    query_grads, shares = [], []
+    query_grads, pairs = [], []
     swap = [(0, 1), (1, 0)]
     block = (n, 2, local_slots, width)
     for c in range(kv_heads // n):
@@ -154,10 +154,11 @@
         flat_grad = (ranks, n * 2 * local_slots, width)
         arrived = lax.ppermute(dother.reshape(flat_grad), "dp", swap)
         pair = (down.reshape(flat_grad) + arrived).astype(jnp.bfloat16)
-        share = lax.psum_scatter(pair, "seq", scatter_dimension=0, tiled=False)
-        shares.append(share.astype(jnp.float32).reshape(block))
+        pairs.append(pair)
+    both = jnp.concatenate(pairs, axis=1)
+    share = lax.psum_scatter(both, "seq", scatter_dimension=0, tiled=False)
+    share = share.astype(jnp.float32).reshape(kv_heads, 2, local_slots, width).transpose(1, 2, 0, 3)
     query_grad = jnp.concatenate(query_grads, axis=1)
-    share = jnp.concatenate(shares, axis=0).transpose(1, 2, 0, 3)
     return (query_grad, share[0] * key_pass, share[1] * value_pass)
 
 

time: 336 us -> 327 us (0.973)
  waiting for transfers between devices: 195 us -> 190 us
  other arithmetic: 18.9 us -> 14.8 us
    all_gather x2, waiting for transfers between devices: 52.1 us -> 102 us  [local(): own = lax.all_gather(flat, 'seq', axis=0, tiled=False)]
    reduce_scatter x2 -> x1, waiting for transfers between devices: 126 us -> 83.5 us  [local(): share = lax.psum_scatter(both, 'seq', scatter_dimension=0, tiled=False)]
    ppermute x2, waiting for transfers between devices: 13.7 us -> 0.01 us  [local(): other = lax.ppermute(own, 'dp', swap)]
    convert_element_type x2, other arithmetic: 9.53 us -> 3.33 us  [local(): pair = (down.reshape(flat_grad) + arrived).astype(jnp.bfloat16)]
  transfers between devices with their start and end apart: 8 -> 7, of which waited for: 6 -> 4; matrix products, arithmetic and copies ran while one was open for 3% -> 1% of each run, Pallas kernels for 30% -> 31%
where the time goes in v4:
time: 327 us
  waiting for transfers between devices  190 us (58%)
  Pallas kernels  101 us (31%)
  other arithmetic  14.8 us (5%)
  between operations  13.9 us (4%)
  local copies, waits for them, and re-layouts  5.93 us (2%)
    all_gather x2, waiting for transfers between devices, local(): own = lax.all_gather(flat, 'seq', axis=0, tiled=False)  102 us
    pallas_call x2, Pallas kernels, attend_call(): pl.pallas_call(functools.partial(attend_kernel, step, group), grid=(pairs...  101 us
    reduce_scatter x1, waiting for transfers between devices, local(): share = lax.psum_scatter(both, 'seq', scatter_dimension=0, tiled=False)  83.5 us
  transfers between devices with their start and end apart: 7, of which 4 were waited for; matrix products, arithmetic and copies ran while one was open for 1% of the time, Pallas kernels for 31%

profile of v4, /device:TPU:0, one launch (start us, length us, event | category | flops | bytes accessed | tf_op | source)
XLA Modules:
  0.0 326.7 jit_solution(17616165291780708959)
XLA Ops:
  7.2 0.0 all-gather.3.cloned.1.call-start
  7.2 0.8 fusion.26
  8.0 3.1 compare_reduce_fusion
  11.1 0.1 copy.32
  11.2 1.9 fusion.10
  13.1 0.1 maximum_bitcast_fusion
  13.2 0.8 fusion.72
  14.0 0.0 all-gather.3.cloned.1.call-update
  14.0 0.0 all-gather.5.cloned.1.call-start
  14.1 0.7 all-gather.5.cloned.1.call-update
  14.8 0.2 reduce-scatter.2.cloned.1.call-start
  15.0 51.2 %all-gather.3.cloned.1.call-done = bf16[8,1024,128]{2,1,0:T(8,128)(2,1)} async-done(((bf16[1,1024,128]{2,1,0:T(8,128)(2,1)}), bf16[8,1024,128]{2,1,0:T(8,128)(2,1)}) %all-gather.3.cloned.1.call-update) | async-done | bytes 2097168 | tf_op jit(solution)/shard_map/all_gather | solution.py:147
  66.2 0.0 collective-permute-start
  66.2 50.5 %all-gather.5.cloned.1.call-done = bf16[8,1024,128]{2,1,0:T(8,128)(2,1)} async-done(((bf16[1,1024,128]{2,1,0:T(8,128)(2,1)}), bf16[8,1024,128]{2,1,0:T(8,128)(2,1)}) %all-gather.5.cloned.1.call-update) | async-done | bytes 2097168 | tf_op jit(solution)/shard_map/all_gather | solution.py:147
  116.7 0.0 collective-permute-start.1
  116.7 0.0 collective-permute-done
  116.7 50.3 %shard_map.85 = (bf16[128,32,128]{2,1,0:T(8,128)(2,1)}, f32[8,4,2,128,128]{4,3,2,1,0:T(8,128)}, f32[8,4,2,128,128]{4,3,2,1,0:T(8,128)}) custom-call(bf16[128,64,128]{2,1,0:T(8,128)(2,1)} %q_ref.3, bf16[128,64,128]{2,1,0:T(8,128)(2,1)} %g_ref.3, bf16[8,4,2,128,128]{4,3,2,1,0:T(8,128)(2,1)} %bitcast.66, bf16[8,4,2,128,128]{4,3,2,1,0:T(8,128)(2,1)} %bitcast.13.other_ref), custom_call_target="tpu_custom_call" | custom-call | flops 21474836480 | bytes 12582912 | tf_op jit(solution)/shard_map/pallas_call | solution.py:105
  167.0 0.5 collective-permute-start.2
  167.5 0.0 collective-permute-done.1
  167.5 0.0 copy-start.6
  167.5 1.3 copy-done.6
  168.8 0.0 copy-start
  168.8 50.5 %shard_map.86 = (bf16[128,32,128]{2,1,0:T(8,128)(2,1)}, f32[8,4,2,128,128]{4,3,2,1,0:T(8,128)}, f32[8,4,2,128,128]{4,3,2,1,0:T(8,128)}) custom-call(bf16[128,64,128]{2,1,0:T(8,128)(2,1)} %q_ref.3, bf16[128,64,128]{2,1,0:T(8,128)(2,1)} %g_ref.3, bf16[8,4,2,128,128]{4,3,2,1,0:T(8,128)(2,1)} %bitcast.65, bf16[8,4,2,128,128]{4,3,2,1,0:T(8,128)(2,1)} %bitcast.67), custom_call_target="tpu_custom_call" | custom-call | flops 21474836480 | bytes 12582912 | tf_op jit(solution)/shard_map/pallas_call | solution.py:105
  219.3 0.0 collective-permute-start.3
  219.3 0.0 collective-permute-done.2
  219.3 0.0 copy-done
  219.3 0.0 copy-start.1
  219.3 2.7 fusion.1
  222.1 4.6 %collective-permute-done.3 = f32[8,1024,128]{2,1,0:T(8,128)S(1)} collective-permute-done((f32[8,1024,128]{2,1,0:T(8,128)}, f32[8,1024,128]{2,1,0:T(8,128)S(1)}, u32[]{:S(2)}, u32[]{:S(2)}) %collective-permute-start.3) | collective-permute-done | bytes 4194336 | tf_op jit(solution)/shard_map/ppermute | solution.py:155
  226.7 0.0 copy-done.1
  226.7 0.6 fusion
  227.3 2.2 pad_maximum_fusion
  229.5 0.0 copy-start.4
  229.5 0.0 copy-start.5
  229.5 0.0 copy-start.2
  229.5 0.0 copy-start.3
  229.5 0.0 reduce-scatter.2.cloned.1.call-update
  229.5 1.2 copy-done.4
  230.7 0.3 copy-done.5
  231.0 1.6 pad_maximum_fusion.1
  232.6 83.5 %reduce-scatter.2.cloned.1.call-done = bf16[1,2048,128]{2,1,0:T(8,128)(2,1)} async-done(((bf16[8,2048,128]{2,1,0:T(8,128)(2,1)}), bf16[1,2048,128]{2,1,0:T(8,128)(2,1)}) %reduce-scatter.2.cloned.1.call-update) | async-done | bytes 524304 | tf_op jit(solution)/shard_map/reduce_scatter | solution.py:159
  316.1 1.1 copy_bitcast_fusion
  317.2 0.0 copy-done.2
  317.2 0.0 copy-done.3
  317.2 0.7 fusion.2
  318.0 1.1 copy.39
  319.1 1.1 copy.40
  (3 shorter events, 0.1 us)
Async XLA Ops:
  7.2 59.0 %all-gather.3.cloned.1.call-start = ((), (), s32[]{:S(2)}) async-start(), calls=%async_computation.1 | async-start | bytes 2359296 | tf_op jit(solution)/shard_map/all_gather | solution.py:147
  14.0 102.7 %all-gather.5.cloned.1.call-start = ((), (), s32[]{:S(2)}) async-start(), calls=%async_computation.2 | async-start | bytes 2359296 | tf_op jit(solution)/shard_map/all_gather | solution.py:147
  14.8 301.3 %reduce-scatter.2.cloned.1.call-start = ((), (), s32[]{:S(2)}) async-start(), calls=%async_computation.3 | async-start | bytes 4718592 | tf_op jit(solution)/shard_map/reduce_scatter | solution.py:159
  66.2 50.5 %collective-permute-start = (bf16[8,1024,128]{2,1,0:T(8,128)(2,1)}, bf16[8,1024,128]{2,1,0:T(8,128)(2,1)}, u32[]{:S(2)}, u32[]{:S(2)}) collective-permute-start(bf16[8,1024,128]{2,1,0:T(8,128)(2,1)} %all-gather.3.cloned.1.call-done), channel_id=1, source_target_pairs={{0,8},{8,0},{1,9},{9,1},{2,10},{10,2},{3,11},{11,3},{4,12},{12,4},... | collective-permute-start | bytes 6291464 | tf_op jit(solution)/shard_map/ppermute | solution.py:148
  116.7 50.8 %collective-permute-start.1 = (bf16[8,1024,128]{2,1,0:T(8,128)(2,1)}, bf16[8,1024,128]{2,1,0:T(8,128)(2,1)S(1)}, u32[]{:S(2)}, u32[]{:S(2)}) collective-permute-start(bf16[8,1024,128]{2,1,0:T(8,128)(2,1)} %all-gather.5.cloned.1.call-done), channel_id=1, source_target_pairs={{0,8},{8,0},{1,9},{9,1},{2,10},{10,2},{3,11},{11,3},{4,12},{12,4},... | collective-permute-start | bytes 6291464 | tf_op jit(solution)/shard_map/ppermute | solution.py:148
  167.0 52.3 %collective-permute-start.2 = (f32[8,1024,128]{2,1,0:T(8,128)}, f32[8,1024,128]{2,1,0:T(8,128)}, u32[]{:S(2)}, u32[]{:S(2)}) collective-permute-start(f32[8,1024,128]{2,1,0:T(8,128)} %bitcast.63), channel_id=1, source_target_pairs={{0,8},{8,0},{1,9},{9,1},{2,10},{10,2},{3,11},{11,3},{4,12},{12,4},... | collective-permute-start | bytes 12582920 | tf_op jit(solution)/shard_map/ppermute | solution.py:155
  167.5 1.3 copy-start.6
  168.8 50.5 %copy-start = (f32[8,4,2,128,128]{4,3,2,1,0:T(8,128)S(1)}, f32[8,4,2,128,128]{4,3,2,1,0:T(8,128)}, u32[]{:S(2)}) copy-start(f32[8,4,2,128,128]{4,3,2,1,0:T(8,128)} %get-tuple-element.11) | copy-start | bytes 12582916
  219.3 7.4 %collective-permute-start.3 = (f32[8,1024,128]{2,1,0:T(8,128)}, f32[8,1024,128]{2,1,0:T(8,128)S(1)}, u32[]{:S(2)}, u32[]{:S(2)}) collective-permute-start(f32[8,1024,128]{2,1,0:T(8,128)} %bitcast.64), channel_id=1, source_target_pairs={{0,8},{8,0},{1,9},{9,1},{2,10},{10,2},{3,11},{11,3},{4,12},{12,4},... | collective-permute-start | bytes 12582920 | tf_op jit(solution)/shard_map/ppermute | solution.py:155
  219.3 7.3 %copy-start.1 = (f32[8,4,2,128,128]{4,3,2,1,0:T(8,128)S(1)}, f32[8,4,2,128,128]{4,3,2,1,0:T(8,128)}, u32[]{:S(2)}) copy-start(f32[8,4,2,128,128]{4,3,2,1,0:T(8,128)} %get-tuple-element.13) | copy-start | bytes 12582916
  229.5 1.2 copy-start.4
  229.5 1.5 copy-start.5
  229.5 87.7 %copy-start.2 = (f32[128,8,128]{2,1,0:T(8,128)S(1)}, f32[128,8,128]{2,1,0:T(8,128)}, u32[]{:S(2)}) copy-start(f32[128,8,128]{2,1,0:T(8,128)} %param.8) | copy-start | bytes 1572868
  229.5 87.7 %copy-start.3 = (f32[128,8,128]{2,1,0:T(8,128)S(1)}, f32[128,8,128]{2,1,0:T(8,128)}, u32[]{:S(2)}) copy-start(f32[128,8,128]{2,1,0:T(8,128)} %param.9) | copy-start | bytes 1572868
Sparse Core Ops, SparseCore 0:
  14.2 51.9 all-gather.2
  68.9 47.7 all-gather.4
  229.6 86.3 reduce-scatter.1
